TPU v7x, 256 devices: a whole 4x4x8 slice. The times are simulated.
256 devices in a mesh: pole: 8 (over y, core), snode: 32 (over x, z).
Axes of the slice: x: 4, y: 4, z: 8, core: 2. Of those that a mesh axis runs over, the one named last changes fastest.
Arguments:
- pivot_inverse: float32 [16, 64, 2, 256, 256], P('pole', 'snode'), as said below
- factor_block: float32 [16, 64, 2, 256, 256], P('pole', 'snode')
- live_width_array: int32 [64], P('snode'), may hold values from 128 to 256, as said below
- pole_weight: float32 [16, 2], P('pole'), may hold values from -4 to 4
Outputs:
- density_diag: float32 [64, 256, 256], P('snode')
- density_off: float32 [64, 256, 256], P('snode')
Inputs may be any that keep to these rules, and one draw needn't show every extreme that they name: `live_width_array`: live widths of the supernodes; at least one supernode is 256 wide and one is 128 wide. `pivot_inverse`: symmetric in its last two dimensions with a dominant real diagonal.
All inputs are finite; a program needn't handle non-finite values.
Results may differ from a plain program's by a relative error of at most 0.0003.
Values sent between devices are 32-bit elements; how exact they have to be, the bound alone decides.
A program may use at most 192 MiB of HBM per device.

v0:
```python
import jax
import jax.numpy as jnp
from jax import lax
from jax.sharding import PartitionSpec as P


def passed_along(value, axis, steps):
    count = lax.axis_size(axis)
    first, last = (max(0, -steps), min(count, count - steps))
    return lax.ppermute(value, axis, [(source, source + steps) for source in range(first, last)])


def multiply_real(left, right):
    return jnp.einsum("...ij,...jk->...ik", left, right, precision=lax.Precision.HIGHEST)


def complex_product(left, right):
    left_real = left[..., 0, :, :]
    leading_imaginary = left[..., 1, :, :]
    right_re = right[..., 0, :, :]
    right_im = right[..., 1, :, :]
    real_part = multiply_real(left_real, right_re) - multiply_real(leading_imaginary, right_im)
    imag_part = multiply_real(left_real, right_im) + multiply_real(leading_imaginary, right_re)
    return jnp.stack([real_part, imag_part], axis=-3)


def transpose_block(block):
    return jnp.swapaxes(block, -1, -2)


def local(pivot_inverse, factor_block, live_width_array, pole_weight):
    width = pivot_inverse.shape[-1]
    local_count = pivot_inverse.shape[1]
    columns = jnp.arange(width, dtype=jnp.int32)
    keep = (columns[None, :] < live_width_array[:, None]).astype(jnp.float32)
    pivot = pivot_inverse * keep[None, :, None, :, None] * keep[None, :, None, None, :]
    factor = factor_block * keep[None, :, None, None, :]

    def sweep_local(parent):
        reciprocal_matrices = []
        offsets = []
        for slot in range(local_count):
            link = factor[:, slot]
            product = complex_product(parent, link)
            parent = pivot[:, slot] + complex_product(transpose_block(link), product)
            reciprocal_matrices.append(parent)
            offsets.append(-product)
        return (jnp.stack(reciprocal_matrices, axis=1), jnp.stack(offsets, axis=1))

    position = lax.axis_index("snode")
    turns = lax.axis_size("snode")

    def one_turn(count, carry):
        reciprocal_matrices, offsets = carry
        incoming = passed_along(reciprocal_matrices[:, -1], "snode", 1)
        return lax.cond(
            position == count, sweep_local, lambda value: (reciprocal_matrices, offsets), incoming
        )

    empty = jnp.zeros(pivot.shape, jnp.float32)
    reciprocal_matrices, offsets = lax.fori_loop(0, turns, one_turn, (empty, empty))
    weight_re = pole_weight[:, 0][:, None, None, None]
    weight_im = pole_weight[:, 1][:, None, None, None]
    diag_local = jnp.sum(
        weight_re * reciprocal_matrices[:, :, 1] + weight_im * reciprocal_matrices[:, :, 0], axis=0
    )
    off_local = jnp.sum(weight_re * offsets[:, :, 1] + weight_im * offsets[:, :, 0], axis=0)
    density_diag, density_off = lax.psum((diag_local, off_local), "pole")
    return (density_diag, density_off)


def solution(mesh):
    placed = (
        P("pole", "snode", None, None, None),
        P("pole", "snode", None, None, None),
        P("snode"),
        P("pole", None),
    )
    return jax.shard_map(
        local,
        mesh=mesh,
        in_specs=placed,
        out_specs=(P("snode", None, None), P("snode", None, None)),
        check_vma=False,
    )
```

profile of v0, /device:TPU:167, one launch (start us, length us, event | category | flops | bytes accessed | tf_op | source)
XLA Modules:
  0.0 1545.9 jit_solution(14331864448455064707)
XLA Ops:
  7.9 4.4 copy_multiply_fusion
  17.5 1400.2 %while.15 = (s32[]{:T(128)}, f32[2,2,2,256,256]{3,4,0,2,1:T(8,128)}, f32[2,2,2,256,256]{4,3,0,2,1:T(8,128)}, s32[]{:T(128)}, f32[2,2,2,256,256]{3,4,0,2,1:T(8,12...) while((s32[]{:T(128)}, f32[2,2,2,256,256]{3,4,0,2,1:T(8,128)}, f32[2,2,2,256,256]{4,3,0,2,1:T(8,128)}, ...), condition=%wide.region_3.0_spmd, body=%wide.region_0.0_spmd.sunk | while | flops 6447169536 | bytes 68157640 | solution.py:61
  25.4 23.5 %collective-permute-done = f32[2,2,256,256]{3,2,0,1:T(8,128)S(1)} collective-permute-done((f32[2,2,256,256]{3,2,0,1:T(8,128)}, f32[2,2,256,256]{3,2,0,1:T(8,128)S(1)}, u32[]{:S(2)}, u32[]{:S(2)}) %collective-permute-start) | collective-permute-done | bytes 1048608 | tf_op jit(solution)/shard_map/while/body/eval_jaxpr/ppermute | solution.py:10
  48.9 2.9 copy.63
  56.8 23.3 %collective-permute-done = f32[2,2,256,256]{3,2,0,1:T(8,128)S(1)} collective-permute-done((f32[2,2,256,256]{3,2,0,1:T(8,128)}, f32[2,2,256,256]{3,2,0,1:T(8,128)S(1)}, u32[]{:S(2)}, u32[]{:S(2)}) %collective-permute-start) | collective-permute-done | bytes 1048608 | tf_op jit(solution)/shard_map/while/body/eval_jaxpr/ppermute | solution.py:10
  80.1 2.9 copy.63
  87.3 23.6 %collective-permute-done = f32[2,2,256,256]{3,2,0,1:T(8,128)S(1)} collective-permute-done((f32[2,2,256,256]{3,2,0,1:T(8,128)}, f32[2,2,256,256]{3,2,0,1:T(8,128)S(1)}, u32[]{:S(2)}, u32[]{:S(2)}) %collective-permute-start) | collective-permute-done | bytes 1048608 | tf_op jit(solution)/shard_map/while/body/eval_jaxpr/ppermute | solution.py:10
  110.9 2.9 copy.63
  118.1 22.6 %collective-permute-done = f32[2,2,256,256]{3,2,0,1:T(8,128)S(1)} collective-permute-done((f32[2,2,256,256]{3,2,0,1:T(8,128)}, f32[2,2,256,256]{3,2,0,1:T(8,128)S(1)}, u32[]{:S(2)}, u32[]{:S(2)}) %collective-permute-start) | collective-permute-done | bytes 1048608 | tf_op jit(solution)/shard_map/while/body/eval_jaxpr/ppermute | solution.py:10
  140.7 2.9 copy.63
  147.9 21.7 %collective-permute-done = f32[2,2,256,256]{3,2,0,1:T(8,128)S(1)} collective-permute-done((f32[2,2,256,256]{3,2,0,1:T(8,128)}, f32[2,2,256,256]{3,2,0,1:T(8,128)S(1)}, u32[]{:S(2)}, u32[]{:S(2)}) %collective-permute-start) | collective-permute-done | bytes 1048608 | tf_op jit(solution)/shard_map/while/body/eval_jaxpr/ppermute | solution.py:10
  169.6 2.9 copy.63
  176.8 20.8 %collective-permute-done = f32[2,2,256,256]{3,2,0,1:T(8,128)S(1)} collective-permute-done((f32[2,2,256,256]{3,2,0,1:T(8,128)}, f32[2,2,256,256]{3,2,0,1:T(8,128)S(1)}, u32[]{:S(2)}, u32[]{:S(2)}) %collective-permute-start) | collective-permute-done | bytes 1048608 | tf_op jit(solution)/shard_map/while/body/eval_jaxpr/ppermute | solution.py:10
  197.6 2.9 copy.63
  204.8 19.9 %collective-permute-done = f32[2,2,256,256]{3,2,0,1:T(8,128)S(1)} collective-permute-done((f32[2,2,256,256]{3,2,0,1:T(8,128)}, f32[2,2,256,256]{3,2,0,1:T(8,128)S(1)}, u32[]{:S(2)}, u32[]{:S(2)}) %collective-permute-start) | collective-permute-done | bytes 1048608 | tf_op jit(solution)/shard_map/while/body/eval_jaxpr/ppermute | solution.py:10
  224.7 2.9 copy.63
  231.9 19.0 %collective-permute-done = f32[2,2,256,256]{3,2,0,1:T(8,128)S(1)} collective-permute-done((f32[2,2,256,256]{3,2,0,1:T(8,128)}, f32[2,2,256,256]{3,2,0,1:T(8,128)S(1)}, u32[]{:S(2)}, u32[]{:S(2)}) %collective-permute-start) | collective-permute-done | bytes 1048608 | tf_op jit(solution)/shard_map/while/body/eval_jaxpr/ppermute | solution.py:10
  250.9 2.9 copy.63
  258.1 18.0 %collective-permute-done = f32[2,2,256,256]{3,2,0,1:T(8,128)S(1)} collective-permute-done((f32[2,2,256,256]{3,2,0,1:T(8,128)}, f32[2,2,256,256]{3,2,0,1:T(8,128)S(1)}, u32[]{:S(2)}, u32[]{:S(2)}) %collective-permute-start) | collective-permute-done | bytes 1048608 | tf_op jit(solution)/shard_map/while/body/eval_jaxpr/ppermute | solution.py:10
  276.1 2.9 copy.63
  283.3 17.1 %collective-permute-done = f32[2,2,256,256]{3,2,0,1:T(8,128)S(1)} collective-permute-done((f32[2,2,256,256]{3,2,0,1:T(8,128)}, f32[2,2,256,256]{3,2,0,1:T(8,128)S(1)}, u32[]{:S(2)}, u32[]{:S(2)}) %collective-permute-start) | collective-permute-done | bytes 1048608 | tf_op jit(solution)/shard_map/while/body/eval_jaxpr/ppermute | solution.py:10
  300.4 2.9 copy.63
  307.6 18.8 %collective-permute-done = f32[2,2,256,256]{3,2,0,1:T(8,128)S(1)} collective-permute-done((f32[2,2,256,256]{3,2,0,1:T(8,128)}, f32[2,2,256,256]{3,2,0,1:T(8,128)S(1)}, u32[]{:S(2)}, u32[]{:S(2)}) %collective-permute-start) | collective-permute-done | bytes 1048608 | tf_op jit(solution)/shard_map/while/body/eval_jaxpr/ppermute | solution.py:10
  326.4 2.9 copy.63
  333.6 17.2 %collective-permute-done = f32[2,2,256,256]{3,2,0,1:T(8,128)S(1)} collective-permute-done((f32[2,2,256,256]{3,2,0,1:T(8,128)}, f32[2,2,256,256]{3,2,0,1:T(8,128)S(1)}, u32[]{:S(2)}, u32[]{:S(2)}) %collective-permute-start) | collective-permute-done | bytes 1048608 | tf_op jit(solution)/shard_map/while/body/eval_jaxpr/ppermute | solution.py:10
  358.0 15.6 %collective-permute-done = f32[2,2,256,256]{3,2,0,1:T(8,128)S(1)} collective-permute-done((f32[2,2,256,256]{3,2,0,1:T(8,128)}, f32[2,2,256,256]{3,2,0,1:T(8,128)S(1)}, u32[]{:S(2)}, u32[]{:S(2)}) %collective-permute-start) | collective-permute-done | bytes 1048608 | tf_op jit(solution)/shard_map/while/body/eval_jaxpr/ppermute | solution.py:10
  380.8 14.8 collective-permute-done
  402.7 15.6 %collective-permute-done = f32[2,2,256,256]{3,2,0,1:T(8,128)S(1)} collective-permute-done((f32[2,2,256,256]{3,2,0,1:T(8,128)}, f32[2,2,256,256]{3,2,0,1:T(8,128)S(1)}, u32[]{:S(2)}, u32[]{:S(2)}) %collective-permute-start) | collective-permute-done | bytes 1048608 | tf_op jit(solution)/shard_map/while/body/eval_jaxpr/ppermute | solution.py:10
  418.3 2.9 copy.63
  425.5 17.0 %collective-permute-done = f32[2,2,256,256]{3,2,0,1:T(8,128)S(1)} collective-permute-done((f32[2,2,256,256]{3,2,0,1:T(8,128)}, f32[2,2,256,256]{3,2,0,1:T(8,128)S(1)}, u32[]{:S(2)}, u32[]{:S(2)}) %collective-permute-start) | collective-permute-done | bytes 1048608 | tf_op jit(solution)/shard_map/while/body/eval_jaxpr/ppermute | solution.py:10
  442.5 2.9 copy.63
  449.7 17.9 %collective-permute-done = f32[2,2,256,256]{3,2,0,1:T(8,128)S(1)} collective-permute-done((f32[2,2,256,256]{3,2,0,1:T(8,128)}, f32[2,2,256,256]{3,2,0,1:T(8,128)S(1)}, u32[]{:S(2)}, u32[]{:S(2)}) %collective-permute-start) | collective-permute-done | bytes 1048608 | tf_op jit(solution)/shard_map/while/body/eval_jaxpr/ppermute | solution.py:10
  467.6 2.9 copy.63
  474.8 18.5 %collective-permute-done = f32[2,2,256,256]{3,2,0,1:T(8,128)S(1)} collective-permute-done((f32[2,2,256,256]{3,2,0,1:T(8,128)}, f32[2,2,256,256]{3,2,0,1:T(8,128)S(1)}, u32[]{:S(2)}, u32[]{:S(2)}) %collective-permute-start) | collective-permute-done | bytes 1048608 | tf_op jit(solution)/shard_map/while/body/eval_jaxpr/ppermute | solution.py:10
  493.3 2.9 copy.63
  500.5 20.5 %collective-permute-done = f32[2,2,256,256]{3,2,0,1:T(8,128)S(1)} collective-permute-done((f32[2,2,256,256]{3,2,0,1:T(8,128)}, f32[2,2,256,256]{3,2,0,1:T(8,128)S(1)}, u32[]{:S(2)}, u32[]{:S(2)}) %collective-permute-start) | collective-permute-done | bytes 1048608 | tf_op jit(solution)/shard_map/while/body/eval_jaxpr/ppermute | solution.py:10
  528.2 22.4 %collective-permute-done = f32[2,2,256,256]{3,2,0,1:T(8,128)S(1)} collective-permute-done((f32[2,2,256,256]{3,2,0,1:T(8,128)}, f32[2,2,256,256]{3,2,0,1:T(8,128)S(1)}, u32[]{:S(2)}, u32[]{:S(2)}) %collective-permute-start) | collective-permute-done | bytes 1048608 | tf_op jit(solution)/shard_map/while/body/eval_jaxpr/ppermute | solution.py:10
  550.6 2.9 copy.63
  557.8 23.5 %collective-permute-done = f32[2,2,256,256]{3,2,0,1:T(8,128)S(1)} collective-permute-done((f32[2,2,256,256]{3,2,0,1:T(8,128)}, f32[2,2,256,256]{3,2,0,1:T(8,128)S(1)}, u32[]{:S(2)}, u32[]{:S(2)}) %collective-permute-start) | collective-permute-done | bytes 1048608 | tf_op jit(solution)/shard_map/while/body/eval_jaxpr/ppermute | solution.py:10
  588.5 24.6 %collective-permute-done = f32[2,2,256,256]{3,2,0,1:T(8,128)S(1)} collective-permute-done((f32[2,2,256,256]{3,2,0,1:T(8,128)}, f32[2,2,256,256]{3,2,0,1:T(8,128)S(1)}, u32[]{:S(2)}, u32[]{:S(2)}) %collective-permute-start) | collective-permute-done | bytes 1048608 | tf_op jit(solution)/shard_map/while/body/eval_jaxpr/ppermute | solution.py:10
  613.1 2.9 copy.63
  620.3 25.7 %collective-permute-done = f32[2,2,256,256]{3,2,0,1:T(8,128)S(1)} collective-permute-done((f32[2,2,256,256]{3,2,0,1:T(8,128)}, f32[2,2,256,256]{3,2,0,1:T(8,128)S(1)}, u32[]{:S(2)}, u32[]{:S(2)}) %collective-permute-start) | collective-permute-done | bytes 1048608 | tf_op jit(solution)/shard_map/while/body/eval_jaxpr/ppermute | solution.py:10
  645.9 2.9 copy.63
  653.1 26.7 %collective-permute-done = f32[2,2,256,256]{3,2,0,1:T(8,128)S(1)} collective-permute-done((f32[2,2,256,256]{3,2,0,1:T(8,128)}, f32[2,2,256,256]{3,2,0,1:T(8,128)S(1)}, u32[]{:S(2)}, u32[]{:S(2)}) %collective-permute-start) | collective-permute-done | bytes 1048608 | tf_op jit(solution)/shard_map/while/body/eval_jaxpr/ppermute | solution.py:10
  679.9 2.9 copy.63
  687.1 27.8 %collective-permute-done = f32[2,2,256,256]{3,2,0,1:T(8,128)S(1)} collective-permute-done((f32[2,2,256,256]{3,2,0,1:T(8,128)}, f32[2,2,256,256]{3,2,0,1:T(8,128)S(1)}, u32[]{:S(2)}, u32[]{:S(2)}) %collective-permute-start) | collective-permute-done | bytes 1048608 | tf_op jit(solution)/shard_map/while/body/eval_jaxpr/ppermute | solution.py:10
  714.9 2.9 copy.63
  722.1 28.4 %collective-permute-done = f32[2,2,256,256]{3,2,0,1:T(8,128)S(1)} collective-permute-done((f32[2,2,256,256]{3,2,0,1:T(8,128)}, f32[2,2,256,256]{3,2,0,1:T(8,128)S(1)}, u32[]{:S(2)}, u32[]{:S(2)}) %collective-permute-start) | collective-permute-done | bytes 1048608 | tf_op jit(solution)/shard_map/while/body/eval_jaxpr/ppermute | solution.py:10
  750.5 2.9 copy.63
  757.7 27.6 %collective-permute-done = f32[2,2,256,256]{3,2,0,1:T(8,128)S(1)} collective-permute-done((f32[2,2,256,256]{3,2,0,1:T(8,128)}, f32[2,2,256,256]{3,2,0,1:T(8,128)S(1)}, u32[]{:S(2)}, u32[]{:S(2)}) %collective-permute-start) | collective-permute-done | bytes 1048608 | tf_op jit(solution)/shard_map/while/body/eval_jaxpr/ppermute | solution.py:10
  785.4 2.9 copy.63
  792.6 25.5 %collective-permute-done = f32[2,2,256,256]{3,2,0,1:T(8,128)S(1)} collective-permute-done((f32[2,2,256,256]{3,2,0,1:T(8,128)}, f32[2,2,256,256]{3,2,0,1:T(8,128)S(1)}, u32[]{:S(2)}, u32[]{:S(2)}) %collective-permute-start) | collective-permute-done | bytes 1048608 | tf_op jit(solution)/shard_map/while/body/eval_jaxpr/ppermute | solution.py:10
  818.1 2.9 copy.63
  825.3 23.7 %collective-permute-done = f32[2,2,256,256]{3,2,0,1:T(8,128)S(1)} collective-permute-done((f32[2,2,256,256]{3,2,0,1:T(8,128)}, f32[2,2,256,256]{3,2,0,1:T(8,128)S(1)}, u32[]{:S(2)}, u32[]{:S(2)}) %collective-permute-start) | collective-permute-done | bytes 1048608 | tf_op jit(solution)/shard_map/while/body/eval_jaxpr/ppermute | solution.py:10
  848.9 2.9 copy.63
  856.1 478.6 %collective-permute-done = f32[2,2,256,256]{3,2,0,1:T(8,128)S(1)} collective-permute-done((f32[2,2,256,256]{3,2,0,1:T(8,128)}, f32[2,2,256,256]{3,2,0,1:T(8,128)S(1)}, u32[]{:S(2)}, u32[]{:S(2)}) %collective-permute-start) | collective-permute-done | bytes 1048608 | tf_op jit(solution)/shard_map/while/body/eval_jaxpr/ppermute | solution.py:10
  1334.7 21.4 %conditional.2 = ((f32[2,2,2,256,256]{3,4,0,2,1:T(8,128)}, f32[2,2,2,256,256]{4,3,0,2,1:T(8,128)})) conditional(s32[]{:T(128)} %convert_element_type.21, (f32[2,2,2,256,256]{3,4,0,2,1:T(8,128)}, f32[2,2,2,256,256]{4,3,0,2,1:T(8,128)}) %tuple.50, (f32[2,2,2,256,256]{3,4,0,2,1:T(8,128)S(1)}, f32[2,2,256,256]{3,2,0,1:T(8,128)S(1)}, ...), branch_computations={%region_1.0_spmd, %region_2.0_spmd} | conditional | flops 6447169536 | bytes 57671704 | solution.py:56
  1363.2 13.8 collective-permute-done
  1377.1 2.9 copy.63
  1382.3 23.3 %collective-permute-start = (f32[2,2,256,256]{3,2,0,1:T(8,128)}, f32[2,2,256,256]{3,2,0,1:T(8,128)S(1)}, u32[]{:S(2)}, u32[]{:S(2)}) collective-permute-start(f32[2,2,256,256]{3,2,0,1:T(8,128)} %slice_bitcast_fusion.39), channel_id=1, source_target_pairs={{0,1},{1,2},{2,3},{3,4},{4,5},{5,6},{6,7},{7,8},{8,9},{9,10},{10,1... | collective-permute-start | bytes 3145736 | tf_op jit(solution)/shard_map/while/body/eval_jaxpr/ppermute | solution.py:10
  1405.6 12.0 collective-permute-done
  1417.7 3.1 copy.31
  1420.7 3.0 fusion.21
  1423.8 111.5 %all-reduce.3.cloned.1.call-done = (f32[2,256,256]{2,1,0:T(8,128)}, f32[2,256,256]{2,1,0:T(8,128)}) async-done(((f32[2,256,256]{2,1,0:T(8,128)}, f32[2,256,256]{2,1,0:T(8,128)}), (f32[2,256,256]{2,1,0:T(8,128)}, f32[2,256,256]{2,1,0:T(8,128)})) %all-reduce.3.cloned.1.call-update) | async-done | bytes 1048592 | tf_op jit(solution)/shard_map/psum | solution.py:68
  (136 shorter events, 187.5 us)
Async XLA Ops:
  7.2 1528.2 %all-reduce.3.cloned.1.call-start = ((), (), s32[]{:S(2)}) async-start(), calls=%async_computation | async-start | bytes 2097152 | tf_op jit(solution)/shard_map/psum | solution.py:68
  12.4 1.9 copy-start.1
  22.8 26.1 %collective-permute-start = (f32[2,2,256,256]{3,2,0,1:T(8,128)}, f32[2,2,256,256]{3,2,0,1:T(8,128)S(1)}, u32[]{:S(2)}, u32[]{:S(2)}) collective-permute-start(f32[2,2,256,256]{3,2,0,1:T(8,128)} %slice_bitcast_fusion.39), channel_id=1, source_target_pairs={{0,1},{1,2},{2,3},{3,4},{4,5},{5,6},{6,7},{7,8},{8,9},{9,10},{10,1... | collective-permute-start | bytes 3145736 | tf_op jit(solution)/shard_map/while/body/eval_jaxpr/ppermute | solution.py:10
  54.2 26.0 %collective-permute-start = (f32[2,2,256,256]{3,2,0,1:T(8,128)}, f32[2,2,256,256]{3,2,0,1:T(8,128)S(1)}, u32[]{:S(2)}, u32[]{:S(2)}) collective-permute-start(f32[2,2,256,256]{3,2,0,1:T(8,128)} %slice_bitcast_fusion.39), channel_id=1, source_target_pairs={{0,1},{1,2},{2,3},{3,4},{4,5},{5,6},{6,7},{7,8},{8,9},{9,10},{10,1... | collective-permute-start | bytes 3145736 | tf_op jit(solution)/shard_map/while/body/eval_jaxpr/ppermute | solution.py:10
  85.4 25.5 %collective-permute-start = (f32[2,2,256,256]{3,2,0,1:T(8,128)}, f32[2,2,256,256]{3,2,0,1:T(8,128)S(1)}, u32[]{:S(2)}, u32[]{:S(2)}) collective-permute-start(f32[2,2,256,256]{3,2,0,1:T(8,128)} %slice_bitcast_fusion.39), channel_id=1, source_target_pairs={{0,1},{1,2},{2,3},{3,4},{4,5},{5,6},{6,7},{7,8},{8,9},{9,10},{10,1... | collective-permute-start | bytes 3145736 | tf_op jit(solution)/shard_map/while/body/eval_jaxpr/ppermute | solution.py:10
  116.2 24.6 %collective-permute-start = (f32[2,2,256,256]{3,2,0,1:T(8,128)}, f32[2,2,256,256]{3,2,0,1:T(8,128)S(1)}, u32[]{:S(2)}, u32[]{:S(2)}) collective-permute-start(f32[2,2,256,256]{3,2,0,1:T(8,128)} %slice_bitcast_fusion.39), channel_id=1, source_target_pairs={{0,1},{1,2},{2,3},{3,4},{4,5},{5,6},{6,7},{7,8},{8,9},{9,10},{10,1... | collective-permute-start | bytes 3145736 | tf_op jit(solution)/shard_map/while/body/eval_jaxpr/ppermute | solution.py:10
  146.0 23.6 %collective-permute-start = (f32[2,2,256,256]{3,2,0,1:T(8,128)}, f32[2,2,256,256]{3,2,0,1:T(8,128)S(1)}, u32[]{:S(2)}, u32[]{:S(2)}) collective-permute-start(f32[2,2,256,256]{3,2,0,1:T(8,128)} %slice_bitcast_fusion.39), channel_id=1, source_target_pairs={{0,1},{1,2},{2,3},{3,4},{4,5},{5,6},{6,7},{7,8},{8,9},{9,10},{10,1... | collective-permute-start | bytes 3145736 | tf_op jit(solution)/shard_map/while/body/eval_jaxpr/ppermute | solution.py:10
  174.9 22.7 %collective-permute-start = (f32[2,2,256,256]{3,2,0,1:T(8,128)}, f32[2,2,256,256]{3,2,0,1:T(8,128)S(1)}, u32[]{:S(2)}, u32[]{:S(2)}) collective-permute-start(f32[2,2,256,256]{3,2,0,1:T(8,128)} %slice_bitcast_fusion.39), channel_id=1, source_target_pairs={{0,1},{1,2},{2,3},{3,4},{4,5},{5,6},{6,7},{7,8},{8,9},{9,10},{10,1... | collective-permute-start | bytes 3145736 | tf_op jit(solution)/shard_map/while/body/eval_jaxpr/ppermute | solution.py:10
  202.9 21.8 %collective-permute-start = (f32[2,2,256,256]{3,2,0,1:T(8,128)}, f32[2,2,256,256]{3,2,0,1:T(8,128)S(1)}, u32[]{:S(2)}, u32[]{:S(2)}) collective-permute-start(f32[2,2,256,256]{3,2,0,1:T(8,128)} %slice_bitcast_fusion.39), channel_id=1, source_target_pairs={{0,1},{1,2},{2,3},{3,4},{4,5},{5,6},{6,7},{7,8},{8,9},{9,10},{10,1... | collective-permute-start | bytes 3145736 | tf_op jit(solution)/shard_map/while/body/eval_jaxpr/ppermute | solution.py:10
  230.0 20.9 %collective-permute-start = (f32[2,2,256,256]{3,2,0,1:T(8,128)}, f32[2,2,256,256]{3,2,0,1:T(8,128)S(1)}, u32[]{:S(2)}, u32[]{:S(2)}) collective-permute-start(f32[2,2,256,256]{3,2,0,1:T(8,128)} %slice_bitcast_fusion.39), channel_id=1, source_target_pairs={{0,1},{1,2},{2,3},{3,4},{4,5},{5,6},{6,7},{7,8},{8,9},{9,10},{10,1... | collective-permute-start | bytes 3145736 | tf_op jit(solution)/shard_map/while/body/eval_jaxpr/ppermute | solution.py:10
  256.2 20.0 %collective-permute-start = (f32[2,2,256,256]{3,2,0,1:T(8,128)}, f32[2,2,256,256]{3,2,0,1:T(8,128)S(1)}, u32[]{:S(2)}, u32[]{:S(2)}) collective-permute-start(f32[2,2,256,256]{3,2,0,1:T(8,128)} %slice_bitcast_fusion.39), channel_id=1, source_target_pairs={{0,1},{1,2},{2,3},{3,4},{4,5},{5,6},{6,7},{7,8},{8,9},{9,10},{10,1... | collective-permute-start | bytes 3145736 | tf_op jit(solution)/shard_map/while/body/eval_jaxpr/ppermute | solution.py:10
  281.4 19.0 %collective-permute-start = (f32[2,2,256,256]{3,2,0,1:T(8,128)}, f32[2,2,256,256]{3,2,0,1:T(8,128)S(1)}, u32[]{:S(2)}, u32[]{:S(2)}) collective-permute-start(f32[2,2,256,256]{3,2,0,1:T(8,128)} %slice_bitcast_fusion.39), channel_id=1, source_target_pairs={{0,1},{1,2},{2,3},{3,4},{4,5},{5,6},{6,7},{7,8},{8,9},{9,10},{10,1... | collective-permute-start | bytes 3145736 | tf_op jit(solution)/shard_map/while/body/eval_jaxpr/ppermute | solution.py:10
  305.7 20.7 %collective-permute-start = (f32[2,2,256,256]{3,2,0,1:T(8,128)}, f32[2,2,256,256]{3,2,0,1:T(8,128)S(1)}, u32[]{:S(2)}, u32[]{:S(2)}) collective-permute-start(f32[2,2,256,256]{3,2,0,1:T(8,128)} %slice_bitcast_fusion.39), channel_id=1, source_target_pairs={{0,1},{1,2},{2,3},{3,4},{4,5},{5,6},{6,7},{7,8},{8,9},{9,10},{10,1... | collective-permute-start | bytes 3145736 | tf_op jit(solution)/shard_map/while/body/eval_jaxpr/ppermute | solution.py:10
  331.7 19.1 %collective-permute-start = (f32[2,2,256,256]{3,2,0,1:T(8,128)}, f32[2,2,256,256]{3,2,0,1:T(8,128)S(1)}, u32[]{:S(2)}, u32[]{:S(2)}) collective-permute-start(f32[2,2,256,256]{3,2,0,1:T(8,128)} %slice_bitcast_fusion.39), channel_id=1, source_target_pairs={{0,1},{1,2},{2,3},{3,4},{4,5},{5,6},{6,7},{7,8},{8,9},{9,10},{10,1... | collective-permute-start | bytes 3145736 | tf_op jit(solution)/shard_map/while/body/eval_jaxpr/ppermute | solution.py:10
  356.1 17.5 %collective-permute-start = (f32[2,2,256,256]{3,2,0,1:T(8,128)}, f32[2,2,256,256]{3,2,0,1:T(8,128)S(1)}, u32[]{:S(2)}, u32[]{:S(2)}) collective-permute-start(f32[2,2,256,256]{3,2,0,1:T(8,128)} %slice_bitcast_fusion.39), channel_id=1, source_target_pairs={{0,1},{1,2},{2,3},{3,4},{4,5},{5,6},{6,7},{7,8},{8,9},{9,10},{10,1... | collective-permute-start | bytes 3145736 | tf_op jit(solution)/shard_map/while/body/eval_jaxpr/ppermute | solution.py:10
  378.9 16.7 %collective-permute-start = (f32[2,2,256,256]{3,2,0,1:T(8,128)}, f32[2,2,256,256]{3,2,0,1:T(8,128)S(1)}, u32[]{:S(2)}, u32[]{:S(2)}) collective-permute-start(f32[2,2,256,256]{3,2,0,1:T(8,128)} %slice_bitcast_fusion.39), channel_id=1, source_target_pairs={{0,1},{1,2},{2,3},{3,4},{4,5},{5,6},{6,7},{7,8},{8,9},{9,10},{10,1... | collective-permute-start | bytes 3145736 | tf_op jit(solution)/shard_map/while/body/eval_jaxpr/ppermute | solution.py:10
  400.8 17.5 %collective-permute-start = (f32[2,2,256,256]{3,2,0,1:T(8,128)}, f32[2,2,256,256]{3,2,0,1:T(8,128)S(1)}, u32[]{:S(2)}, u32[]{:S(2)}) collective-permute-start(f32[2,2,256,256]{3,2,0,1:T(8,128)} %slice_bitcast_fusion.39), channel_id=1, source_target_pairs={{0,1},{1,2},{2,3},{3,4},{4,5},{5,6},{6,7},{7,8},{8,9},{9,10},{10,1... | collective-permute-start | bytes 3145736 | tf_op jit(solution)/shard_map/while/body/eval_jaxpr/ppermute | solution.py:10
  423.6 18.9 %collective-permute-start = (f32[2,2,256,256]{3,2,0,1:T(8,128)}, f32[2,2,256,256]{3,2,0,1:T(8,128)S(1)}, u32[]{:S(2)}, u32[]{:S(2)}) collective-permute-start(f32[2,2,256,256]{3,2,0,1:T(8,128)} %slice_bitcast_fusion.39), channel_id=1, source_target_pairs={{0,1},{1,2},{2,3},{3,4},{4,5},{5,6},{6,7},{7,8},{8,9},{9,10},{10,1... | collective-permute-start | bytes 3145736 | tf_op jit(solution)/shard_map/while/body/eval_jaxpr/ppermute | solution.py:10
  447.8 19.8 %collective-permute-start = (f32[2,2,256,256]{3,2,0,1:T(8,128)}, f32[2,2,256,256]{3,2,0,1:T(8,128)S(1)}, u32[]{:S(2)}, u32[]{:S(2)}) collective-permute-start(f32[2,2,256,256]{3,2,0,1:T(8,128)} %slice_bitcast_fusion.39), channel_id=1, source_target_pairs={{0,1},{1,2},{2,3},{3,4},{4,5},{5,6},{6,7},{7,8},{8,9},{9,10},{10,1... | collective-permute-start | bytes 3145736 | tf_op jit(solution)/shard_map/while/body/eval_jaxpr/ppermute | solution.py:10
  472.9 20.5 %collective-permute-start = (f32[2,2,256,256]{3,2,0,1:T(8,128)}, f32[2,2,256,256]{3,2,0,1:T(8,128)S(1)}, u32[]{:S(2)}, u32[]{:S(2)}) collective-permute-start(f32[2,2,256,256]{3,2,0,1:T(8,128)} %slice_bitcast_fusion.39), channel_id=1, source_target_pairs={{0,1},{1,2},{2,3},{3,4},{4,5},{5,6},{6,7},{7,8},{8,9},{9,10},{10,1... | collective-permute-start | bytes 3145736 | tf_op jit(solution)/shard_map/while/body/eval_jaxpr/ppermute | solution.py:10
  498.6 22.4 %collective-permute-start = (f32[2,2,256,256]{3,2,0,1:T(8,128)}, f32[2,2,256,256]{3,2,0,1:T(8,128)S(1)}, u32[]{:S(2)}, u32[]{:S(2)}) collective-permute-start(f32[2,2,256,256]{3,2,0,1:T(8,128)} %slice_bitcast_fusion.39), channel_id=1, source_target_pairs={{0,1},{1,2},{2,3},{3,4},{4,5},{5,6},{6,7},{7,8},{8,9},{9,10},{10,1... | collective-permute-start | bytes 3145736 | tf_op jit(solution)/shard_map/while/body/eval_jaxpr/ppermute | solution.py:10
  526.3 24.3 %collective-permute-start = (f32[2,2,256,256]{3,2,0,1:T(8,128)}, f32[2,2,256,256]{3,2,0,1:T(8,128)S(1)}, u32[]{:S(2)}, u32[]{:S(2)}) collective-permute-start(f32[2,2,256,256]{3,2,0,1:T(8,128)} %slice_bitcast_fusion.39), channel_id=1, source_target_pairs={{0,1},{1,2},{2,3},{3,4},{4,5},{5,6},{6,7},{7,8},{8,9},{9,10},{10,1... | collective-permute-start | bytes 3145736 | tf_op jit(solution)/shard_map/while/body/eval_jaxpr/ppermute | solution.py:10
  555.9 25.4 %collective-permute-start = (f32[2,2,256,256]{3,2,0,1:T(8,128)}, f32[2,2,256,256]{3,2,0,1:T(8,128)S(1)}, u32[]{:S(2)}, u32[]{:S(2)}) collective-permute-start(f32[2,2,256,256]{3,2,0,1:T(8,128)} %slice_bitcast_fusion.39), channel_id=1, source_target_pairs={{0,1},{1,2},{2,3},{3,4},{4,5},{5,6},{6,7},{7,8},{8,9},{9,10},{10,1... | collective-permute-start | bytes 3145736 | tf_op jit(solution)/shard_map/while/body/eval_jaxpr/ppermute | solution.py:10
  586.6 26.5 %collective-permute-start = (f32[2,2,256,256]{3,2,0,1:T(8,128)}, f32[2,2,256,256]{3,2,0,1:T(8,128)S(1)}, u32[]{:S(2)}, u32[]{:S(2)}) collective-permute-start(f32[2,2,256,256]{3,2,0,1:T(8,128)} %slice_bitcast_fusion.39), channel_id=1, source_target_pairs={{0,1},{1,2},{2,3},{3,4},{4,5},{5,6},{6,7},{7,8},{8,9},{9,10},{10,1... | collective-permute-start | bytes 3145736 | tf_op jit(solution)/shard_map/while/body/eval_jaxpr/ppermute | solution.py:10
  618.3 27.6 %collective-permute-start = (f32[2,2,256,256]{3,2,0,1:T(8,128)}, f32[2,2,256,256]{3,2,0,1:T(8,128)S(1)}, u32[]{:S(2)}, u32[]{:S(2)}) collective-permute-start(f32[2,2,256,256]{3,2,0,1:T(8,128)} %slice_bitcast_fusion.39), channel_id=1, source_target_pairs={{0,1},{1,2},{2,3},{3,4},{4,5},{5,6},{6,7},{7,8},{8,9},{9,10},{10,1... | collective-permute-start | bytes 3145736 | tf_op jit(solution)/shard_map/while/body/eval_jaxpr/ppermute | solution.py:10
  651.2 28.7 %collective-permute-start = (f32[2,2,256,256]{3,2,0,1:T(8,128)}, f32[2,2,256,256]{3,2,0,1:T(8,128)S(1)}, u32[]{:S(2)}, u32[]{:S(2)}) collective-permute-start(f32[2,2,256,256]{3,2,0,1:T(8,128)} %slice_bitcast_fusion.39), channel_id=1, source_target_pairs={{0,1},{1,2},{2,3},{3,4},{4,5},{5,6},{6,7},{7,8},{8,9},{9,10},{10,1... | collective-permute-start | bytes 3145736 | tf_op jit(solution)/shard_map/while/body/eval_jaxpr/ppermute | solution.py:10
  685.1 29.7 %collective-permute-start = (f32[2,2,256,256]{3,2,0,1:T(8,128)}, f32[2,2,256,256]{3,2,0,1:T(8,128)S(1)}, u32[]{:S(2)}, u32[]{:S(2)}) collective-permute-start(f32[2,2,256,256]{3,2,0,1:T(8,128)} %slice_bitcast_fusion.39), channel_id=1, source_target_pairs={{0,1},{1,2},{2,3},{3,4},{4,5},{5,6},{6,7},{7,8},{8,9},{9,10},{10,1... | collective-permute-start | bytes 3145736 | tf_op jit(solution)/shard_map/while/body/eval_jaxpr/ppermute | solution.py:10
  720.2 30.4 %collective-permute-start = (f32[2,2,256,256]{3,2,0,1:T(8,128)}, f32[2,2,256,256]{3,2,0,1:T(8,128)S(1)}, u32[]{:S(2)}, u32[]{:S(2)}) collective-permute-start(f32[2,2,256,256]{3,2,0,1:T(8,128)} %slice_bitcast_fusion.39), channel_id=1, source_target_pairs={{0,1},{1,2},{2,3},{3,4},{4,5},{5,6},{6,7},{7,8},{8,9},{9,10},{10,1... | collective-permute-start | bytes 3145736 | tf_op jit(solution)/shard_map/while/body/eval_jaxpr/ppermute | solution.py:10
  755.8 29.5 %collective-permute-start = (f32[2,2,256,256]{3,2,0,1:T(8,128)}, f32[2,2,256,256]{3,2,0,1:T(8,128)S(1)}, u32[]{:S(2)}, u32[]{:S(2)}) collective-permute-start(f32[2,2,256,256]{3,2,0,1:T(8,128)} %slice_bitcast_fusion.39), channel_id=1, source_target_pairs={{0,1},{1,2},{2,3},{3,4},{4,5},{5,6},{6,7},{7,8},{8,9},{9,10},{10,1... | collective-permute-start | bytes 3145736 | tf_op jit(solution)/shard_map/while/body/eval_jaxpr/ppermute | solution.py:10
  790.6 27.4 %collective-permute-start = (f32[2,2,256,256]{3,2,0,1:T(8,128)}, f32[2,2,256,256]{3,2,0,1:T(8,128)S(1)}, u32[]{:S(2)}, u32[]{:S(2)}) collective-permute-start(f32[2,2,256,256]{3,2,0,1:T(8,128)} %slice_bitcast_fusion.39), channel_id=1, source_target_pairs={{0,1},{1,2},{2,3},{3,4},{4,5},{5,6},{6,7},{7,8},{8,9},{9,10},{10,1... | collective-permute-start | bytes 3145736 | tf_op jit(solution)/shard_map/while/body/eval_jaxpr/ppermute | solution.py:10
  823.4 25.6 %collective-permute-start = (f32[2,2,256,256]{3,2,0,1:T(8,128)}, f32[2,2,256,256]{3,2,0,1:T(8,128)S(1)}, u32[]{:S(2)}, u32[]{:S(2)}) collective-permute-start(f32[2,2,256,256]{3,2,0,1:T(8,128)} %slice_bitcast_fusion.39), channel_id=1, source_target_pairs={{0,1},{1,2},{2,3},{3,4},{4,5},{5,6},{6,7},{7,8},{8,9},{9,10},{10,1... | collective-permute-start | bytes 3145736 | tf_op jit(solution)/shard_map/while/body/eval_jaxpr/ppermute | solution.py:10
  854.2 480.5 %collective-permute-start = (f32[2,2,256,256]{3,2,0,1:T(8,128)}, f32[2,2,256,256]{3,2,0,1:T(8,128)S(1)}, u32[]{:S(2)}, u32[]{:S(2)}) collective-permute-start(f32[2,2,256,256]{3,2,0,1:T(8,128)} %slice_bitcast_fusion.39), channel_id=1, source_target_pairs={{0,1},{1,2},{2,3},{3,4},{4,5},{5,6},{6,7},{7,8},{8,9},{9,10},{10,1... | collective-permute-start | bytes 3145736 | tf_op jit(solution)/shard_map/while/body/eval_jaxpr/ppermute | solution.py:10
  1361.3 15.7 %collective-permute-start = (f32[2,2,256,256]{3,2,0,1:T(8,128)}, f32[2,2,256,256]{3,2,0,1:T(8,128)S(1)}, u32[]{:S(2)}, u32[]{:S(2)}) collective-permute-start(f32[2,2,256,256]{3,2,0,1:T(8,128)} %slice_bitcast_fusion.39), channel_id=1, source_target_pairs={{0,1},{1,2},{2,3},{3,4},{4,5},{5,6},{6,7},{7,8},{8,9},{9,10},{10,1... | collective-permute-start | bytes 3145736 | tf_op jit(solution)/shard_map/while/body/eval_jaxpr/ppermute | solution.py:10
  1382.3 35.3 %collective-permute-start = (f32[2,2,256,256]{3,2,0,1:T(8,128)}, f32[2,2,256,256]{3,2,0,1:T(8,128)S(1)}, u32[]{:S(2)}, u32[]{:S(2)}) collective-permute-start(f32[2,2,256,256]{3,2,0,1:T(8,128)} %slice_bitcast_fusion.39), channel_id=1, source_target_pairs={{0,1},{1,2},{2,3},{3,4},{4,5},{5,6},{6,7},{7,8},{8,9},{9,10},{10,1... | collective-permute-start | bytes 3145736 | tf_op jit(solution)/shard_map/while/body/eval_jaxpr/ppermute | solution.py:10
  1417.7 3.1 copy-start
Sparse Core Ops, SparseCore 0:
  1423.9 111.3 all-reduce.2
where the time goes:
time: 1550 us
  waiting for transfers between devices  1240 us (80%)
  local copies, waits for them, and re-layouts  183 us (12%)
  starting transfers between devices  83.9 us (5%)
    ppermute x32, waiting for transfers between devices, passed_along(): lax.ppermute(value, axis, [(source, source + steps) for source in range(f...  1130 us
    psum x1, waiting for transfers between devices, local(): density_diag, density_off = lax.psum((diag_local, off_local), 'pole')  112 us
    another operation x32, local copies, waits for them, and re-layouts  93.1 us
    ppermute x32, starting transfers between devices, passed_along(): lax.ppermute(value, axis, [(source, source + steps) for source in range(f...  83.9 us
    squeeze x32, local copies, waits for them, and re-layouts, one_turn(): incoming = passed_along(reciprocal_matrices[:, -1], 'snode', 1)  75.7 us
  transfers between devices with their start and end apart: 33, of which 33 were waited for; matrix products, arithmetic and copies ran while one was open for 0% of the time, Pallas kernels for 0%

commit v1 on v0

v1 whole, which is shorter than its diff:
```python
import functools

import jax
import jax.numpy as jnp
from jax import lax
from jax.experimental import pallas as pl
from jax.experimental.pallas import tpu as pltpu
from jax.sharding import PartitionSpec as P

MESH = pl.DeviceIdType.MESH
F32 = jnp.float32
BF = jnp.bfloat16
W = 256
H = 128
PACK = 264
PART = 104
ROWS = 8 * PART
CHUNKS = 4
CROWS = W // CHUNKS
GROUP = 4


def split(x):
    high = x.astype(BF)
    return high, (x - high.astype(F32)).astype(BF)


def csplit(pair):
    return split(pair[0]) + split(pair[1])


def dot(a, b):
    return jnp.dot(a, b, preferred_element_type=F32)


def dot_t(a, b):
    return lax.dot_general(a, b, (((0,), (0,)), ((), ())), preferred_element_type=F32)


def product(left, right, mul=dot):
    lrh, lrl, lih, lil = left
    rrh, rrl, rih, ril = right
    real = mul(lrh, rrh) - mul(lih, rih)
    real += (mul(lrl, rrh) + mul(lrh, rrl)) - (mul(lil, rih) + mul(lih, ril))
    imag = mul(lrh, rih) + mul(lih, rrh)
    imag += (mul(lrl, rih) + mul(lrh, ril)) + (mul(lil, rrh) + mul(lih, rrl))
    return real, imag


def sandwich(middle, outer):
    return product(outer, csplit(product(csplit(middle), outer)), dot_t)


def tri():
    row = lax.broadcasted_iota(jnp.int32, (H, H), 0)
    col = lax.broadcasted_iota(jnp.int32, (H, H), 1)
    return row, col


def pack_into(ref, block):
    row, col = tri()
    last = block[H:, H:]
    ref[0:H, :] = block[:H, H:]
    ref[H : 2 * H, :] = jnp.where(row <= col, block[:H, :H], last)
    diagonal = jnp.sum(jnp.where(row == col, last, 0.0), axis=0, keepdims=True)
    ref[2 * H : PACK, :] = jnp.broadcast_to(diagonal, (8, H))


def unpack(ref):
    row, col = tri()
    upper = ref[0:H, :]
    both = ref[H : 2 * H, :]
    both_t = both.T
    diagonal = ref[2 * H : 2 * H + 1, :]
    first = jnp.where(row <= col, both, both_t)
    last = jnp.where(row > col, both, jnp.where(row == col, diagonal, both_t))
    return jnp.concatenate(
        [jnp.concatenate([first, upper], 1), jnp.concatenate([upper.T, last], 1)], 0
    )


def unpack2(ref):
    return unpack(ref.at[0]), unpack(ref.at[1])


def pack2(ref, pair):
    pack_into(ref.at[0], pair[0])
    pack_into(ref.at[1], pair[1])


def kernel(
    nodes,
    width_ref,
    weight_ref,
    p_ref,
    f_ref,
    diag_ref,
    off_ref,
    fs,
    a_s,
    b_own,
    a_ex,
    a_exs,
    a_in,
    a_ins,
    b_ex,
    b_in,
    b_full,
    s_got,
    s_out,
    s_in,
    dens,
    parts,
    total,
    spare,
    b_send,
    b_recv,
    a_send,
    a_recv,
    s_send,
    s_recv,
    rs_send,
    rs_recv,
    ag_send,
    ag_recv,
):
    me = lax.axis_index("pole")
    i = lax.axis_index("snode")
    groups = nodes // GROUP
    g = lax.rem(i, GROUP)
    m = lax.div(i, GROUP)
    head = g == GROUP - 1
    poles = range(2)

    barrier = pltpu.get_barrier_semaphore()
    for step in range(1, GROUP + 1):
        for near in (lax.rem(i + step, nodes), lax.rem(i + nodes - step, nodes)):
            pl.semaphore_signal(barrier, inc=1, device_id=(me, near), device_id_type=MESH)
    for step in range(1, 8):
        pl.semaphore_signal(
            barrier, inc=1, device_id=(lax.rem(me + step, 8), i), device_id_type=MESH
        )

    row = lax.broadcasted_iota(jnp.int32, (W, W), 0)
    col = lax.broadcasted_iota(jnp.int32, (W, W), 1)

    def pivot(p, k):
        live = (row < width_ref[k]) & (col < width_ref[k])
        return tuple(jnp.where(live, p_ref[p, k, part], 0.0) for part in range(2))

    def load4(ref):
        return tuple(ref[n] for n in range(4))

    def store4(ref, four):
        for n in range(4):
            ref[n] = four[n]

    def send_b(p):
        return pltpu.make_async_remote_copy(
            src_ref=b_in.at[p],
            dst_ref=b_ex.at[p],
            send_sem=b_send.at[p],
            recv_sem=b_recv.at[p],
            device_id=(me, lax.rem(i + 1, nodes)),
            device_id_type=MESH,
        )

    def send_a(p, c):
        rows = pl.ds(c * CROWS, CROWS)
        return pltpu.make_async_remote_copy(
            src_ref=a_in.at[p, :, rows],
            dst_ref=a_ex.at[p, :, rows],
            send_sem=a_send.at[p, c],
            recv_sem=a_recv.at[p, c],
            device_id=(me, lax.rem(i + 1, nodes)),
            device_id_type=MESH,
        )

    def send_s(p, ahead, src):
        return pltpu.make_async_remote_copy(
            src_ref=src.at[p],
            dst_ref=s_got.at[p],
            send_sem=s_send.at[p, ahead - 1],
            recv_sem=s_recv.at[p],
            device_id=(me, lax.rem(i + ahead, nodes)),
            device_id_type=MESH,
        )

    def send_state(p, src):
        for ahead in (GROUP,) + tuple(range(1, GROUP)):
            send_s(p, ahead, src).start()

    for p in poles:
        for k in range(2):
            live = col < width_ref[k]
            store4(
                fs.at[p, k],
                csplit([jnp.where(live, f_ref[p, k, part], 0.0) for part in range(2)]),
            )
        outer = load4(fs.at[p, 1])
        inner = sandwich(pivot(p, 0), outer)
        last = pivot(p, 1)
        for part in range(2):
            b_own[p, part] = last[part] + inner[part]

        @pl.when(g == 0)
        def _():
            pack2(b_in.at[p], (b_own[p, 0], b_own[p, 1]))

        if p == 0:
            pl.semaphore_wait(barrier, 2 * GROUP + 7)

        @pl.when(g == 0)
        def _():
            send_b(p).start()

    for p in poles:
        real, imag = product(load4(fs.at[p, 0]), load4(fs.at[p, 1]))
        store4(a_s.at[p], csplit((real, imag)))

        @pl.when((g == 0) & (m > 0))
        def _():
            a_in[p, 0] = real
            a_in[p, 1] = imag
            for c in range(CHUNKS):
                send_a(p, c).start()

    @pl.when(g > 0)
    def _():
        for p in poles:
            send_b(p).wait_recv()
            outer = load4(a_s.at[p])
            inner = sandwich(unpack2(b_ex.at[p]), outer)
            full = (b_own[p, 0] + inner[0], b_own[p, 1] + inner[1])
            pack2(b_in.at[p], full)

            @pl.when(~head)
            def _():
                send_b(p).start()

            @pl.when(head & (m == 0))
            def _():
                send_state(p, b_in)

            b_full[p, 0] = full[0]
            b_full[p, 1] = full[1]

    @pl.when((g > 0) & (m > 0))
    def _():
        for p in poles:
            outer = load4(a_s.at[p])
            for c in range(CHUNKS):
                rows = pl.ds(c * CROWS, CROWS)
                send_a(p, c).wait_recv()
                left = csplit((a_ex[p, 0, rows], a_ex[p, 1, rows]))
                for n in range(4):
                    a_exs[p, n, rows] = left[n]
                real, imag = product(left, outer)

                @pl.when(~head)
                def _():
                    a_in[p, 0, rows] = real
                    a_in[p, 1, rows] = imag
                    send_a(p, c).start()

                @pl.when(head)
                def _():
                    four = csplit((real, imag))
                    for n in range(4):
                        a_ins[p, n, rows] = four[n]

    @pl.when(m > 0)
    def _():
        for p in poles:
            send_s(p, 1, s_out).wait_recv()

            @pl.when(head & (m < groups - 1))
            def _():
                inner = sandwich(unpack2(s_got.at[p]), load4(a_ins.at[p]))
                pack2(s_out.at[p], (b_full[p, 0] + inner[0], b_full[p, 1] + inner[1]))
                send_state(p, s_out)

    def send_part(k, step):
        to = lax.rem(me + step, 8)
        return pltpu.make_async_remote_copy(
            src_ref=dens.at[k, pl.ds(pl.multiple_of(to * PART, 8), PART)],
            dst_ref=parts.at[k, step - 1],
            send_sem=rs_send.at[k, step - 1],
            recv_sem=rs_recv.at[k, step - 1],
            device_id=(to, i),
            device_id_type=MESH,
        )

    def send_total(k, step):
        to = lax.rem(me + step, 8)
        rows = pl.ds(pl.multiple_of(me * PART, 8), PART)
        return pltpu.make_async_remote_copy(
            src_ref=total.at[k, rows],
            dst_ref=total.at[k, rows],
            send_sem=ag_send.at[k, step - 1],
            recv_sem=ag_recv.at[k, step - 1],
            device_id=(to, i),
            device_id_type=MESH,
        )

    order = (4, 3, 5, 2, 6, 7, 1)

    def put(p, k, product_pair, inverse_pair):
        re_w, im_w = weight_ref[p, 0], weight_ref[p, 1]
        off = -(re_w * product_pair[1] + im_w * product_pair[0])
        diag = re_w * inverse_pair[1] + im_w * inverse_pair[0]
        mine = dens.at[k]
        if p == 0:
            mine[0:W, :] = off[:, :H]
            mine[W : 2 * W, :] = off[:, H:]
            pack_into(mine.at[pl.ds(2 * W, PACK)], diag)
            mine[2 * W + PACK : ROWS, :] = jnp.zeros((ROWS - 2 * W - PACK, H), F32)
        else:
            mine[0:W, :] += off[:, :H]
            mine[W : 2 * W, :] += off[:, H:]
            pack_into(spare, diag)
            mine[2 * W : 2 * W + PACK, :] += spare[...]
            for step in order:
                send_part(k, step).start()

    for p in poles:

        @pl.when(m == 0)
        def _():
            @pl.when(g == 0)
            def _():
                s_in[...] = jnp.zeros_like(s_in)

            @pl.when(g > 0)
            def _():
                got = unpack2(b_ex.at[p])
                s_in[0] = got[0]
                s_in[1] = got[1]

        @pl.when(m > 0)
        def _():
            got = unpack2(s_got.at[p])

            @pl.when(g == 0)
            def _():
                s_in[0] = got[0]
                s_in[1] = got[1]

            @pl.when(g > 0)
            def _():
                inner = sandwich(got, load4(a_exs.at[p]))
                base = unpack2(b_ex.at[p])
                s_in[0] = base[0] + inner[0]
                s_in[1] = base[1] + inner[1]

        state = (s_in[0], s_in[1])
        for k in range(2):
            link = load4(fs.at[p, k])
            moved = product(csplit(state), link)
            inner = product(link, csplit(moved), dot_t)
            block = pivot(p, k)
            state = (block[0] + inner[0], block[1] + inner[1])
            put(p, k, moved, state)

    mine = pl.ds(pl.multiple_of(me * PART, 8), PART)
    for k in range(2):
        acc = dens[k, mine]
        for step in range(1, 8):
            send_part(k, step).wait_recv()
            acc = acc + parts[k, step - 1]
        total[k, mine] = acc
        for step in order:
            send_total(k, step).start()
    for k in range(2):
        for step in range(1, 8):
            back = lax.rem(me + 8 - step, 8)
            rows = pl.ds(pl.multiple_of(back * PART, 8), PART)
            pltpu.make_async_remote_copy(
                src_ref=total.at[k, rows],
                dst_ref=total.at[k, rows],
                send_sem=ag_send.at[k, step - 1],
                recv_sem=ag_recv.at[k, step - 1],
                device_id=(back, i),
                device_id_type=MESH,
            ).wait_recv()
        off_ref[k, :, 0:H] = total[k, 0:W]
        off_ref[k, :, H:W] = total[k, W : 2 * W]
        diag_ref[k] = unpack(total.at[k, pl.ds(2 * W, PACK)])

    for p in poles:

        @pl.when(~head)
        def _():
            send_b(p).wait_send()

        @pl.when(~head & (m > 0))
        def _():
            for c in range(CHUNKS):
                send_a(p, c).wait_send()

        @pl.when(head & (m < groups - 1))
        def _():
            for ahead in range(1, GROUP + 1):
                send_s(p, ahead, s_out).wait_send()

    for k in range(2):
        for step in range(1, 8):
            send_part(k, step).wait_send()
            send_total(k, step).wait_send()


def local(nodes, pivot_inverse, factor_block, live_width_array, pole_weight):
    vmem = pl.BlockSpec(memory_space=pltpu.VMEM)
    smem = pl.BlockSpec(memory_space=pltpu.SMEM)
    dma = pltpu.SemaphoreType.DMA
    return pl.pallas_call(
        functools.partial(kernel, nodes),
        out_shape=[jax.ShapeDtypeStruct((2, W, W), F32)] * 2,
        in_specs=[smem, smem, vmem, vmem],
        out_specs=[vmem, vmem],
        scratch_shapes=[
            pltpu.VMEM((2, 2, 4, W, W), BF),
            pltpu.VMEM((2, 4, W, W), BF),
            pltpu.VMEM((2, 2, W, W), F32),
            pltpu.VMEM((2, 2, W, W), F32),
            pltpu.VMEM((2, 4, W, W), BF),
            pltpu.VMEM((2, 2, W, W), F32),
            pltpu.VMEM((2, 4, W, W), BF),
            pltpu.VMEM((2, 2, PACK, H), F32),
            pltpu.VMEM((2, 2, PACK, H), F32),
            pltpu.VMEM((2, 2, W, W), F32),
            pltpu.VMEM((2, 2, PACK, H), F32),
            pltpu.VMEM((2, 2, PACK, H), F32),
            pltpu.VMEM((2, W, W), F32),
            pltpu.VMEM((2, ROWS, H), F32),
            pltpu.VMEM((2, 7, PART, H), F32),
            pltpu.VMEM((2, ROWS, H), F32),
            pltpu.VMEM((PACK, H), F32),
            dma((2,)),
            dma((2,)),
            dma((2, CHUNKS)),
            dma((2, CHUNKS)),
            dma((2, GROUP)),
            dma((2,)),
            dma((2, 7)),
            dma((2, 7)),
            dma((2, 7)),
            dma((2, 7)),
        ],
        compiler_params=pltpu.CompilerParams(
            collective_id=0, has_side_effects=True, vmem_limit_bytes=48 << 20
        ),
        name="selected_inversion",
    )(live_width_array, pole_weight, pivot_inverse, factor_block)


def solution(mesh):
    placed = (
        P("pole", "snode", None, None, None),
        P("pole", "snode", None, None, None),
        P("snode"),
        P("pole", None),
    )
    return jax.shard_map(
        functools.partial(local, mesh.shape["snode"]),
        mesh=mesh,
        in_specs=placed,
        out_specs=(P("snode", None, None), P("snode", None, None)),
        check_vma=False,
    )
```

time: 1550 us -> 187 us (0.12)
  waiting for transfers between devices: 1240 us -> 0 us
  Pallas kernels: 0 us -> 177 us
  local copies, waits for them, and re-layouts: 183 us -> 6.1 us
  starting transfers between devices: 83.9 us -> 0 us
    ppermute x32 -> x0, waiting for transfers between devices: 1130 us -> none  [passed_along(): lax.ppermute(value, axis, [(source, source + steps) for source in range(f...]
    pallas_call x0 -> x1, Pallas kernels: none -> 177 us  [local(): pl.pallas_call(functools.partial(kernel, nodes), out_shape=[jax.ShapeDtyp...]
    psum x1 -> x0, waiting for transfers between devices: 112 us -> none  [local(): density_diag, density_off = lax.psum((diag_local, off_local), 'pole')]
    another operation x32 -> x0, local copies, waits for them, and re-layouts: 93.1 us -> none
    ppermute x32 -> x0, starting transfers between devices: 83.9 us -> none  [passed_along(): lax.ppermute(value, axis, [(source, source + steps) for source in range(f...]
    squeeze x32 -> x0, local copies, waits for them, and re-layouts: 75.7 us -> none  [one_turn(): incoming = passed_along(reciprocal_matrices[:, -1], 'snode', 1)]
  transfers between devices with their start and end apart: 33 -> 0, of which waited for: 33 -> 0; matrix products, arithmetic and copies ran while one was open for 0% -> 0% of each run, Pallas kernels for 0% -> 0%
where the time goes in v1:
time: 187 us; the launch traced here: 184 us
  Pallas kernels  177 us (95%)
  local copies, waits for them, and re-layouts  6.1 us (3%)
    pallas_call x1, Pallas kernels, local(): pl.pallas_call(functools.partial(kernel, nodes), out_shape=[jax.ShapeDtyp...  177 us
    unnamed x10, local copies, waits for them, and re-layouts  6.1 us

profile of v1, /device:TPU:167, one launch (start us, length us, event | category | flops | bytes accessed | tf_op | source)
XLA Modules:
  0.0 183.5 jit_solution(12683923416832984127)
XLA Ops:
  0.6 0.0 copy-start
  0.6 1.6 copy-done
  2.2 0.0 copy-start.1
  2.2 1.6 copy-done.1
  3.8 0.0 copy-start.2
  3.8 0.7 copy-done.2
  4.5 0.0 copy-start.3
  4.5 0.7 copy-done.3
  5.1 176.8 %selected_inversion.1 = (f32[2,256,256]{2,1,0:T(8,128)S(1)}, f32[2,256,256]{2,1,0:T(8,128)S(1)}) custom-call(s32[2]{0:T(128)S(1)} %copy-done.3, f32[2,2]{1,0:T(2,128)S(1)} %copy-done.2, f32[2,2,2,256,256]{4,3,2,1,0:T(8,128)S(1)} %copy-done, f32[2,2,2,256,256]{4,3,2,1,0:T(8,128)S(1)} %copy-done.1), custom_call_target="tpu_custom_call" | custom-call | tf_op jit(solution)/shard_map/selected_inversion/pallas_call | solution.py:416
  182.0 0.8 copy.8
  182.8 0.8 copy.9
Async XLA Ops:
  0.6 1.6 copy-start
  2.2 1.6 copy-start.1
  3.8 0.7 copy-start.2
  4.5 0.7 copy-start.3

commit v2 on v1

v2 whole, which is shorter than its diff:
```python
import functools

import jax
import jax.numpy as jnp
from jax import lax
from jax.experimental import pallas as pl
from jax.experimental.pallas import tpu as pltpu
from jax.sharding import PartitionSpec as P

MESH = pl.DeviceIdType.MESH
F32 = jnp.float32
BF = jnp.bfloat16
W = 256
H = 128
PACK = 264
PART = 104
ROWS = 8 * PART
GROUP = 4
OWN, GOT1, PAIR, GOT2, QUAD, GOT3, OCT = range(7)
NEAR = (1, 2, 4, 5, 7, 8)


def split(x):
    high = x.astype(BF)
    return high, (x - high.astype(F32)).astype(BF)


def csplit(pair):
    return split(pair[0]) + split(pair[1])


def dot(a, b):
    return jnp.dot(a, b, preferred_element_type=F32)


def dot_t(a, b):
    return lax.dot_general(a, b, (((0,), (0,)), ((), ())), preferred_element_type=F32)


def product(left, right, mul=dot):
    lrh, lrl, lih, lil = left
    rrh, rrl, rih, ril = right
    real = mul(lrh, rrh) - mul(lih, rih)
    real += (mul(lrl, rrh) + mul(lrh, rrl)) - (mul(lil, rih) + mul(lih, ril))
    imag = mul(lrh, rih) + mul(lih, rrh)
    imag += (mul(lrl, rih) + mul(lrh, ril)) + (mul(lil, rrh) + mul(lih, rrl))
    return real, imag


def sandwich(middle, outer):
    return product(outer, csplit(product(csplit(middle), outer)), dot_t)


def tri():
    row = lax.broadcasted_iota(jnp.int32, (H, H), 0)
    col = lax.broadcasted_iota(jnp.int32, (H, H), 1)
    return row, col


def pack_into(ref, block):
    row, col = tri()
    last = block[H:, H:]
    ref[0:H, :] = block[:H, H:]
    ref[H : 2 * H, :] = jnp.where(row <= col, block[:H, :H], last)
    diagonal = jnp.sum(jnp.where(row == col, last, 0.0), axis=0, keepdims=True)
    ref[2 * H : PACK, :] = jnp.broadcast_to(diagonal, (8, H))


def unpack(ref):
    row, col = tri()
    upper = ref[0:H, :]
    both = ref[H : 2 * H, :]
    both_t = both.T
    diagonal = ref[2 * H : 2 * H + 1, :]
    first = jnp.where(row <= col, both, both_t)
    last = jnp.where(row > col, both, jnp.where(row == col, diagonal, both_t))
    return jnp.concatenate(
        [jnp.concatenate([first, upper], 1), jnp.concatenate([upper.T, last], 1)], 0
    )


def unpack2(ref):
    return unpack(ref.at[0]), unpack(ref.at[1])


def pack2(ref, pair):
    pack_into(ref.at[0], pair[0])
    pack_into(ref.at[1], pair[1])


def kernel(
    nodes,
    width_hbm,
    weight_hbm,
    p_hbm,
    f_hbm,
    diag_ref,
    off_ref,
    p_ref,
    f_ref,
    width_ref,
    weight_ref,
    fs,
    steps_a,
    steps_b,
    got_a,
    got_b,
    out_a,
    out_b,
    jump,
    entry,
    head_out,
    pair_out,
    own_out,
    s_in,
    dens,
    parts,
    total,
    spare,
    load_sem,
    sent,
    got,
    rs_send,
    rs_recv,
    ag_send,
    ag_recv,
):
    me = lax.axis_index("pole")
    i = lax.axis_index("snode")
    groups = nodes // GROUP
    g = lax.rem(i, GROUP)
    m = lax.div(i, GROUP)
    low = 1 - lax.rem(m, 2)

    loads = [
        pltpu.make_async_copy(width_hbm, width_ref, load_sem.at[0]),
        pltpu.make_async_copy(weight_hbm, weight_ref, load_sem.at[1]),
    ]
    for p in range(2):
        loads.append(pltpu.make_async_copy(f_hbm.at[p], f_ref.at[p], load_sem.at[2 + 2 * p]))
        loads.append(pltpu.make_async_copy(p_hbm.at[p], p_ref.at[p], load_sem.at[3 + 2 * p]))
    for load in loads:
        load.start()

    barrier = pltpu.get_barrier_semaphore()
    for step in NEAR:
        for near in (lax.rem(i + step, nodes), lax.rem(i + nodes - step, nodes)):
            pl.semaphore_signal(barrier, inc=1, device_id=(me, near), device_id_type=MESH)
    for step in range(1, 8):
        pl.semaphore_signal(
            barrier, inc=1, device_id=(lax.rem(me + step, 8), i), device_id_type=MESH
        )

    row = lax.broadcasted_iota(jnp.int32, (W, W), 0)
    col = lax.broadcasted_iota(jnp.int32, (W, W), 1)

    def pivot(p, k):
        live = (row < width_ref[k]) & (col < width_ref[k])
        return tuple(jnp.where(live, p_ref[p, k, part], 0.0) for part in range(2))

    def load4(ref):
        return tuple(ref[n] for n in range(4))

    def store4(ref, four):
        for n in range(4):
            ref[n] = four[n]

    def both(body):
        def turn(n, carry):
            body(n)
            return carry

        lax.fori_loop(0, 2, turn, 0)

    def plus(p, low=low):
        return lax.rem(p + low, 2) == 1

    def first_sender(p):
        return lax.rem(g + lax.rem(p + low, 2), 2) == 1

    def second_sender(p):
        return (plus(p) & (g == 1)) | (~plus(p) & (g == 2))

    def head(p):
        return (plus(p) & (g == 3)) | (~plus(p) & (g == 0))

    composing = m > 0
    quads = composing & (m < groups - 1)
    lower = (low == 1) & quads & (m < groups - 2)
    upper = (low == 0) & quads & (m > 1)

    def remote(src, dst, p, kind, landing, to):
        return pltpu.make_async_remote_copy(
            src_ref=src,
            dst_ref=dst,
            send_sem=sent.at[p, kind],
            recv_sem=got.at[p, landing],
            device_id=(me, to),
            device_id_type=MESH,
        )

    def step_copies(p, level):
        out = jnp.int32(0) if level < 2 else jnp.int32(1)
        way = jnp.where(plus(p), 1, -1)
        if level == 2:
            to = jnp.where(plus(p), i + 1, i + 7)
        else:
            to = i + way * (level + 1)
        to = lax.rem(to + nodes, nodes)
        return [
            remote(out_a.at[p, out], got_a.at[p, level], p, 2 * (level // 2), 2 * level, to),
            remote(out_b.at[p, out], got_b.at[p, level], p, 2 * (level // 2) + 1, 2 * level + 1, to),
        ]

    def post_step(p, level, slot, a_pair):
        out = 0 if level < 2 else 1
        out_a[p, out, 0] = a_pair[0]
        out_a[p, out, 1] = a_pair[1]
        pack2(out_b.at[p, out], (steps_b[p, slot, 0], steps_b[p, slot, 1]))
        for copy in step_copies(p, level):
            copy.start()

    def head_copies(p, src):
        n = m + 1
        forward = lax.rem(p + 1 - lax.rem(n, 2), 2) == 1
        skip = (n == 2) | (n == 4)
        octs = (n == 3) | (n == 5)
        base = lax.rem(GROUP * n, nodes)
        after = lax.rem(GROUP * (n + 1) + 3 * p, nodes)
        real = n < groups
        return [
            (real & skip, remote(src.at[p], jump.at[p], p, 4, 6, after)),
            (real & forward & ~octs & (n < groups - 1), remote(src.at[p], jump.at[p], p, 5, 6, base + 3)),
            (real & forward, remote(src.at[p], jump.at[p], p, 6, 6, base + 1)),
            (real, remote(src.at[p], entry.at[p], p, 7, 7, base)),
        ]

    def send_head(p, src):
        for when, copy in head_copies(p, src):
            pl.when(when)(copy.start)

    def pair_copy(p, ahead):
        return remote(pair_out.at[p], entry.at[p], p, 8, 7, lax.rem(i + ahead, nodes))

    def own_copy(p):
        return remote(own_out.at[p], entry.at[p], p, 9, 7, lax.rem(i + 1, nodes))

    with jax.named_scope("own_steps"):
        loads[0].wait()
        for p in range(2):
            loads[2 + 2 * p].wait()
            for k in range(2):
                live = col < width_ref[k]
                store4(
                    fs.at[p, k],
                    csplit([jnp.where(live, f_ref[p, k, part], 0.0) for part in range(2)]),
                )
            real, imag = product(load4(fs.at[p, 0]), load4(fs.at[p, 1]))
            store4(steps_a.at[p, OWN], csplit((real, imag)))
            loads[3 + 2 * p].wait()
            inner = sandwich(pivot(p, 0), load4(fs.at[p, 1]))
            last = pivot(p, 1)
            for part in range(2):
                steps_b[p, OWN, part] = last[part] + inner[part]

            if p == 0:
                pl.semaphore_wait(barrier, 2 * len(NEAR) + 7)

            @pl.when(composing & first_sender(p))
            def _():
                post_step(p, 0, OWN, (real, imag))

    def merge(p, level, own, received, new, forward):
        for copy in step_copies(p, level):
            copy.wait_recv()
        store4(steps_a.at[p, received], csplit((got_a[p, level, 0], got_a[p, level, 1])))
        block = unpack2(got_b.at[p, level])
        steps_b[p, received, 0] = block[0]
        steps_b[p, received, 1] = block[1]
        first = jnp.where(forward, received, own)
        second = jnp.where(forward, own, received)
        outer = load4(steps_a.at[p, second])
        inner = sandwich((steps_b[p, first, 0], steps_b[p, first, 1]), outer)
        for part in range(2):
            steps_b[p, new, part] = steps_b[p, second, part] + inner[part]
        a_pair = product(load4(steps_a.at[p, first]), outer)
        store4(steps_a.at[p, new], csplit(a_pair))
        return a_pair

    with jax.named_scope("pairs"):

        @pl.when(composing)
        def _():
            def body(p):
                @pl.when(~first_sender(p))
                def _():
                    a_pair = merge(p, 0, OWN, GOT1, PAIR, plus(p))

                    @pl.when(quads & second_sender(p))
                    def _():
                        post_step(p, 1, PAIR, a_pair)

            both(body)

    with jax.named_scope("quads"):

        @pl.when(quads)
        def _():
            def body(p):
                @pl.when(head(p))
                def _():
                    a_pair = merge(p, 1, PAIR, GOT2, QUAD, plus(p))

                    @pl.when(lower)
                    def _():
                        post_step(p, 2, QUAD, a_pair)

            both(body)

    with jax.named_scope("octs"):

        @pl.when(upper)
        def _():
            def body(p):
                @pl.when(head(p))
                def _():
                    merge(p, 2, QUAD, GOT3, OCT, True)

            both(body)

    def advance(p, slot, state, ref):
        inner = sandwich(state, load4(steps_a.at[p, slot]))
        pack2(ref, (steps_b[p, slot, 0] + inner[0], steps_b[p, slot, 1] + inner[1]))

    def jumps(p):
        forward = plus(p) & ((g == 1) | ((g == 3) & quads))
        return composing & (forward | (upper & head(p)))

    with jax.named_scope("jumps"):

        def body(p):
            @pl.when(jumps(p))
            def _():
                remote(jump.at[p], jump.at[p], p, 4, 6, i).wait_recv()
                state = unpack2(jump.at[p])

                @pl.when(g == 1)
                def _():
                    advance(p, PAIR, state, pair_out.at[p])
                    pair_copy(p, 1).start()

                @pl.when(g != 1)
                def _():
                    advance(p, jnp.where(upper, OCT, QUAD), state, head_out.at[p])
                    send_head(p, head_out)

        both(body)

    def send_part(k, step):
        to = lax.rem(me + step, 8)
        return pltpu.make_async_remote_copy(
            src_ref=dens.at[k, pl.ds(pl.multiple_of(to * PART, 8), PART)],
            dst_ref=parts.at[k, step - 1],
            send_sem=rs_send.at[k, step - 1],
            recv_sem=rs_recv.at[k, step - 1],
            device_id=(to, i),
            device_id_type=MESH,
        )

    def send_total(k, step):
        to = lax.rem(me + step, 8)
        rows = pl.ds(pl.multiple_of(me * PART, 8), PART)
        return pltpu.make_async_remote_copy(
            src_ref=total.at[k, rows],
            dst_ref=total.at[k, rows],
            send_sem=ag_send.at[k, step - 1],
            recv_sem=ag_recv.at[k, step - 1],
            device_id=(to, i),
            device_id_type=MESH,
        )

    order = (4, 3, 5, 2, 6, 7, 1)

    def put(n, p, k, product_pair, inverse_pair):
        re_w, im_w = weight_ref[p, 0], weight_ref[p, 1]
        off = -(re_w * product_pair[1] + im_w * product_pair[0])
        diag = re_w * inverse_pair[1] + im_w * inverse_pair[0]
        mine = dens.at[k]
        if n == 0:
            mine[0:W, :] = off[:, :H]
            mine[W : 2 * W, :] = off[:, H:]
            pack_into(mine.at[pl.ds(2 * W, PACK)], diag)
            mine[2 * W + PACK : ROWS, :] = jnp.zeros((ROWS - 2 * W - PACK, H), F32)
        else:
            mine[0:W, :] += off[:, :H]
            mine[W : 2 * W, :] += off[:, H:]
            pack_into(spare, diag)
            mine[2 * W : 2 * W + PACK, :] += spare[...]
            for step in order:
                send_part(k, step).start()

    loads[1].wait()
    passes_on = (m == 0) | (lax.rem(g, 2) == 0)
    with jax.named_scope("states"):
        for n in range(2):
            p = lax.rem(low + n, 2)

            @pl.when(i == 0)
            def _():
                s_in[...] = jnp.zeros_like(s_in)

            @pl.when(i > 0)
            def _():
                remote(entry.at[p], entry.at[p], p, 7, 7, i).wait_recv()
                block = unpack2(entry.at[p])
                s_in[0] = block[0]
                s_in[1] = block[1]

            @pl.when(composing & (g == 0) & ~plus(p))
            def _():
                @pl.when(quads & ~upper)
                def _():
                    advance(p, QUAD, (s_in[0], s_in[1]), head_out.at[p])
                    send_head(p, head_out)

                advance(p, PAIR, (s_in[0], s_in[1]), pair_out.at[p])
                pair_copy(p, 2).start()

            @pl.when(passes_on)
            def _():
                advance(p, OWN, (s_in[0], s_in[1]), own_out.at[p])

                @pl.when((m > 0) | (g < 3))
                def _():
                    own_copy(p).start()

                @pl.when((m == 0) & (g == 3))
                def _():
                    send_head(p, own_out)

            state = (s_in[0], s_in[1])
            for k in range(2):
                link = load4(fs.at[p, k])
                moved = product(csplit(state), link)
                inner = product(link, csplit(moved), dot_t)
                block = pivot(p, k)
                state = (block[0] + inner[0], block[1] + inner[1])
                put(n, p, k, moved, state)

    with jax.named_scope("pole_sum"):
        mine = pl.ds(pl.multiple_of(me * PART, 8), PART)
        for k in range(2):
            acc = dens[k, mine]
            for step in range(1, 8):
                send_part(k, step).wait_recv()
                acc = acc + parts[k, step - 1]
            total[k, mine] = acc
            for step in order:
                send_total(k, step).start()
    with jax.named_scope("pole_gather"):
        for k in range(2):
            for step in range(1, 8):
                back = lax.rem(me + 8 - step, 8)
                rows = pl.ds(pl.multiple_of(back * PART, 8), PART)
                pltpu.make_async_remote_copy(
                    src_ref=total.at[k, rows],
                    dst_ref=total.at[k, rows],
                    send_sem=ag_send.at[k, step - 1],
                    recv_sem=ag_recv.at[k, step - 1],
                    device_id=(back, i),
                    device_id_type=MESH,
                ).wait_recv()
            off_ref[k, :, 0:H] = total[k, 0:W]
            off_ref[k, :, H:W] = total[k, W : 2 * W]
            diag_ref[k] = unpack(total.at[k, pl.ds(2 * W, PACK)])

    def body(p):
        @pl.when(composing & (first_sender(p) | (quads & second_sender(p))))
        def _():
            for copy in step_copies(p, 0):
                copy.wait_send()

        @pl.when(lower & head(p))
        def _():
            for copy in step_copies(p, 2):
                copy.wait_send()

        @pl.when((quads & head(p)) | ((m == 0) & (g == 3)))
        def _():
            for when, copy in head_copies(p, head_out):
                pl.when(when)(copy.wait_send)

        @pl.when(composing & ((plus(p) & (g == 1)) | (~plus(p) & (g == 0))))
        def _():
            pair_copy(p, 1).wait_send()

        @pl.when(passes_on & ((m > 0) | (g < 3)))
        def _():
            own_copy(p).wait_send()

    both(body)
    for k in range(2):
        for step in range(1, 8):
            send_part(k, step).wait_send()
            send_total(k, step).wait_send()


def local(nodes, pivot_inverse, factor_block, live_width_array, pole_weight):
    vmem = pl.BlockSpec(memory_space=pltpu.VMEM)
    hbm = pl.BlockSpec(memory_space=pl.ANY)
    dma = pltpu.SemaphoreType.DMA
    packed = pltpu.VMEM((2, 2, PACK, H), F32)
    return pl.pallas_call(
        functools.partial(kernel, nodes),
        out_shape=[jax.ShapeDtypeStruct((2, W, W), F32)] * 2,
        in_specs=[hbm, hbm, hbm, hbm],
        out_specs=[vmem, vmem],
        scratch_shapes=[
            pltpu.VMEM((2, 2, 2, W, W), F32),
            pltpu.VMEM((2, 2, 2, W, W), F32),
            pltpu.SMEM((2,), jnp.int32),
            pltpu.SMEM((2, 2), F32),
            pltpu.VMEM((2, 2, 4, W, W), BF),
            pltpu.VMEM((2, 7, 4, W, W), BF),
            pltpu.VMEM((2, 7, 2, W, W), F32),
            pltpu.VMEM((2, 3, 2, W, W), F32),
            pltpu.VMEM((2, 3, 2, PACK, H), F32),
            pltpu.VMEM((2, 2, 2, W, W), F32),
            pltpu.VMEM((2, 2, 2, PACK, H), F32),
            packed,
            packed,
            packed,
            packed,
            packed,
            pltpu.VMEM((2, W, W), F32),
            pltpu.VMEM((2, ROWS, H), F32),
            pltpu.VMEM((2, 7, PART, H), F32),
            pltpu.VMEM((2, ROWS, H), F32),
            pltpu.VMEM((PACK, H), F32),
            dma((6,)),
            dma((2, 10)),
            dma((2, 8)),
            dma((2, 7)),
            dma((2, 7)),
            dma((2, 7)),
            dma((2, 7)),
        ],
        compiler_params=pltpu.CompilerParams(
            collective_id=0, has_side_effects=True, vmem_limit_bytes=44 << 20
        ),
        name="selected_inversion",
    )(live_width_array, pole_weight, pivot_inverse, factor_block)


def solution(mesh):
    placed = (
        P("pole", "snode", None, None, None),
        P("pole", "snode", None, None, None),
        P("snode"),
        P("pole", None),
    )
    return jax.shard_map(
        functools.partial(local, mesh.shape["snode"]),
        mesh=mesh,
        in_specs=placed,
        out_specs=(P("snode", None, None), P("snode", None, None)),
        check_vma=False,
    )
```

time: 187 us -> 138 us (0.74)
  the two profiles are of different devices: /device:TPU:167 before, /device:TPU:230 now
where the time goes in v2:
time: 138 us
  Pallas kernels  131 us (95%)
  local copies, waits for them, and re-layouts  6.1 us (4%)
    pallas_call x1, Pallas kernels, local(): pl.pallas_call(functools.partial(kernel, nodes), out_shape=[jax.ShapeDtyp...  131 us
    unnamed x10, local copies, waits for them, and re-layouts  6.1 us

profile of v2, /device:TPU:230, one launch (start us, length us, event | category | flops | bytes accessed | tf_op | source)
XLA Modules:
  0.0 138.2 jit_solution(13016084568703065148)
XLA Ops:
  0.6 0.0 copy-start
  0.6 1.6 %copy-done = f32[2,2,2,256,256]{4,3,2,1,0:T(8,128)S(1)} copy-done((f32[2,2,2,256,256]{4,3,2,1,0:T(8,128)S(1)}, f32[2,2,2,256,256]{4,3,2,1,0:T(8,128)}, u32[]{:S(2)}) %copy-start) | copy-done | bytes 2097176
  2.2 0.0 copy-start.1
  2.2 1.6 %copy-done.1 = f32[2,2,2,256,256]{4,3,2,1,0:T(8,128)S(1)} copy-done((f32[2,2,2,256,256]{4,3,2,1,0:T(8,128)S(1)}, f32[2,2,2,256,256]{4,3,2,1,0:T(8,128)}, u32[]{:S(2)}) %copy-start.1) | copy-done | bytes 2097176
  3.8 0.0 copy-start.2
  3.8 0.7 copy-done.2
  4.5 0.0 copy-start.3
  4.5 0.7 copy-done.3
  5.1 131.4 %selected_inversion.1 = (f32[2,256,256]{2,1,0:T(8,128)S(1)}, f32[2,256,256]{2,1,0:T(8,128)S(1)}) custom-call(s32[2]{0:T(128)S(1)} %copy-done.3, f32[2,2]{1,0:T(2,128)S(1)} %copy-done.2, f32[2,2,2,256,256]{4,3,2,1,0:T(8,128)S(1)} %copy-done, f32[2,2,2,256,256]{4,3,2,1,0:T(8,128)S(1)} %copy-done.1), custom_call_target="tpu_custom_call" | custom-call | tf_op jit(solution)/shard_map/selected_inversion/pallas_call | solution.py:513
  136.6 0.8 copy.8
  137.4 0.8 copy.9
Async XLA Ops:
  0.6 1.6 %copy-start = (f32[2,2,2,256,256]{4,3,2,1,0:T(8,128)S(1)}, f32[2,2,2,256,256]{4,3,2,1,0:T(8,128)}, u32[]{:S(2)}) copy-start(f32[2,2,2,256,256]{4,3,2,1,0:T(8,128)} %p_hbm.1) | copy-start | bytes 6291460
  2.2 1.6 %copy-start.1 = (f32[2,2,2,256,256]{4,3,2,1,0:T(8,128)S(1)}, f32[2,2,2,256,256]{4,3,2,1,0:T(8,128)}, u32[]{:S(2)}) copy-start(f32[2,2,2,256,256]{4,3,2,1,0:T(8,128)} %f_hbm.1) | copy-start | bytes 6291460
  3.8 0.7 copy-start.2
  4.5 0.7 copy-start.3

commit v3 on v2

--- a/solution.py
+++ b/solution.py
@@ -16,6 +16,7 @@
 PART = 104
 ROWS = 8 * PART
 GROUP = 4
+VMEM_MIB = 52
 OWN, GOT1, PAIR, GOT2, QUAD, GOT3, OCT = range(7)
 NEAR = (1, 2, 4, 5, 7, 8)
 
@@ -186,8 +187,8 @@
 
     composing = m > 0
     quads = composing & (m < groups - 1)
-    lower = (low == 1) & quads & (m < groups - 2)
-    upper = (low == 0) & quads & (m > 1)
+    lower = m == 4
+    upper = m == 5
 
     def remote(src, dst, p, kind, landing, to):
         return pltpu.make_async_remote_copy(
@@ -223,20 +224,38 @@
     def head_copies(p, src):
         n = m + 1
         forward = lax.rem(p + 1 - lax.rem(n, 2), 2) == 1
-        skip = (n == 2) | (n == 4)
-        octs = (n == 3) | (n == 5)
         base = lax.rem(GROUP * n, nodes)
         after = lax.rem(GROUP * (n + 1) + 3 * p, nodes)
-        real = n < groups
-        return [
-            (real & skip, remote(src.at[p], jump.at[p], p, 4, 6, after)),
-            (real & forward & ~octs & (n < groups - 1), remote(src.at[p], jump.at[p], p, 5, 6, base + 3)),
-            (real & forward, remote(src.at[p], jump.at[p], p, 6, 6, base + 1)),
-            (real, remote(src.at[p], entry.at[p], p, 7, 7, base)),
+        to_oct = n == 4
+        to_head = forward & (n != 5) & (n < groups - 1)
+        to_pair = forward & (n < groups)
+        to_base = n < groups
+        oct_copy = remote(src.at[p], jump.at[p], p, 4, 6, after)
+        head_copy = remote(src.at[p], jump.at[p], p, 5, 6, base + 3)
+        pair = remote(src.at[p], jump.at[p], p, 6, 6, base + 1)
+        base_copy = remote(src.at[p], entry.at[p], p, 7, 7, base)
+        urgent = [
+            (to_oct, oct_copy),
+            (to_head & ~to_oct, head_copy),
+            (to_pair & ~to_head & ~to_oct, pair),
+            (to_base & ~to_pair & ~to_oct, base_copy),
         ]
+        rest = [
+            (to_head & to_oct, head_copy),
+            (to_pair & (to_head | to_oct), pair),
+            (to_base & (to_pair | to_oct), base_copy),
+        ]
+        return urgent, rest
 
     def send_head(p, src):
-        for when, copy in head_copies(p, src):
+        for when, copy in head_copies(p, src)[0]:
+            pl.when(when)(copy.start)
+
+    def send_rest(p, src):
+        urgent, rest = head_copies(p, src)
+        for when, copy in urgent:
+            pl.when(when)(copy.wait_send)
+        for when, copy in rest:
             pl.when(when)(copy.start)
 
     def pair_copy(p, ahead):
@@ -353,6 +372,7 @@
                 def _():
                     advance(p, jnp.where(upper, OCT, QUAD), state, head_out.at[p])
                     send_head(p, head_out)
+                    send_rest(p, head_out)
 
         both(body)
 
@@ -401,51 +421,74 @@
 
     loads[1].wait()
     passes_on = (m == 0) | (lax.rem(g, 2) == 0)
+
+    def enter(p):
+        @pl.when(i == 0)
+        def _():
+            s_in[p] = jnp.zeros_like(s_in[p])
+            pack2(own_out.at[p], (steps_b[p, OWN, 0], steps_b[p, OWN, 1]))
+            own_copy(p).start()
+
+        @pl.when(i > 0)
+        def _():
+            remote(entry.at[p], entry.at[p], p, 7, 7, i).wait_recv()
+            block = unpack2(entry.at[p])
+            s_in[p, 0] = block[0]
+            s_in[p, 1] = block[1]
+
+        @pl.when(composing & (g == 0) & ~plus(p))
+        def _():
+            @pl.when(quads & ~upper)
+            def _():
+                advance(p, QUAD, (s_in[p, 0], s_in[p, 1]), head_out.at[p])
+                send_head(p, head_out)
+
+            advance(p, PAIR, (s_in[p, 0], s_in[p, 1]), pair_out.at[p])
+            pair_copy(p, 2).start()
+
+        @pl.when(passes_on & (i > 0))
+        def _():
+            advance(p, OWN, (s_in[p, 0], s_in[p, 1]), own_out.at[p])
+
+            @pl.when((m > 0) | (g < 3))
+            def _():
+                own_copy(p).start()
+
+            @pl.when((m == 0) & (g == 3))
+            def _():
+                send_head(p, own_out)
+                send_rest(p, own_out)
+
+        @pl.when(quads & ~upper & (g == 0) & ~plus(p))
+        def _():
+            send_rest(p, head_out)
+
+    def details(n, p):
+        state = (s_in[p, 0], s_in[p, 1])
+        for k in range(2):
+            link = load4(fs.at[p, k])
+            moved = product(csplit(state), link)
+            inner = product(link, csplit(moved), dot_t)
+            block = pivot(p, k)
+            state = (block[0] + inner[0], block[1] + inner[1])
+            put(n, p, k, moved, state)
+
     with jax.named_scope("states"):
-        for n in range(2):
-            p = lax.rem(low + n, 2)
-
-            @pl.when(i == 0)
-            def _():
-                s_in[...] = jnp.zeros_like(s_in)
-
-            @pl.when(i > 0)
-            def _():
-                remote(entry.at[p], entry.at[p], p, 7, 7, i).wait_recv()
-                block = unpack2(entry.at[p])
-                s_in[0] = block[0]
-                s_in[1] = block[1]
-
-            @pl.when(composing & (g == 0) & ~plus(p))
-            def _():
-                @pl.when(quads & ~upper)
-                def _():
-                    advance(p, QUAD, (s_in[0], s_in[1]), head_out.at[p])
-                    send_head(p, head_out)
-
-                advance(p, PAIR, (s_in[0], s_in[1]), pair_out.at[p])
-                pair_copy(p, 2).start()
-
-            @pl.when(passes_on)
-            def _():
-                advance(p, OWN, (s_in[0], s_in[1]), own_out.at[p])
-
-                @pl.when((m > 0) | (g < 3))
-                def _():
-                    own_copy(p).start()
-
-                @pl.when((m == 0) & (g == 3))
-                def _():
-                    send_head(p, own_out)
-
-            state = (s_in[0], s_in[1])
-            for k in range(2):
-                link = load4(fs.at[p, k])
-                moved = product(csplit(state), link)
-                inner = product(link, csplit(moved), dot_t)
-                block = pivot(p, k)
-                state = (block[0] + inner[0], block[1] + inner[1])
-                put(n, p, k, moved, state)
+        one, two = lax.rem(low, 2), lax.rem(low + 1, 2)
+        enter(one)
+
+        @pl.when(~passes_on)
+        def _():
+            details(0, one)
+
+        enter(two)
+
+        @pl.when(passes_on)
+        def _():
+            details(0, one)
+
+    with jax.named_scope("last_details"):
+        details(1, two)
 
     with jax.named_scope("pole_sum"):
         mine = pl.ds(pl.multiple_of(me * PART, 8), PART)
@@ -487,7 +530,7 @@
 
         @pl.when((quads & head(p)) | ((m == 0) & (g == 3)))
         def _():
-            for when, copy in head_copies(p, head_out):
+            for when, copy in head_copies(p, head_out)[1]:
                 pl.when(when)(copy.wait_send)
 
         @pl.when(composing & ((plus(p) & (g == 1)) | (~plus(p) & (g == 0))))
@@ -532,7 +575,7 @@
             packed,
             packed,
             packed,
-            pltpu.VMEM((2, W, W), F32),
+            pltpu.VMEM((2, 2, W, W), F32),
             pltpu.VMEM((2, ROWS, H), F32),
             pltpu.VMEM((2, 7, PART, H), F32),
             pltpu.VMEM((2, ROWS, H), F32),
@@ -546,7 +589,7 @@
             dma((2, 7)),
         ],
         compiler_params=pltpu.CompilerParams(
-            collective_id=0, has_side_effects=True, vmem_limit_bytes=44 << 20
+            collective_id=0, has_side_effects=True, vmem_limit_bytes=VMEM_MIB << 20
         ),
         name="selected_inversion",
     )(live_width_array, pole_weight, pivot_inverse, factor_block)

time: 138 us -> 130 us (0.942)
  the two profiles are of different devices: /device:TPU:230 before, /device:TPU:167 now
where the time goes in v3:
time: 130 us; the launch traced here: 127 us
  Pallas kernels  124 us (95%)
  local copies, waits for them, and re-layouts  2.92 us (2%)
    pallas_call x1, Pallas kernels, local(): pl.pallas_call(functools.partial(kernel, nodes), out_shape=[jax.ShapeDtyp...  124 us
    unnamed x6, local copies, waits for them, and re-layouts  2.92 us

profile of v3, /device:TPU:167, one launch (start us, length us, event | category | flops | bytes accessed | tf_op | source)
XLA Modules:
  0.0 127.4 jit_solution(14804950488901221424)
XLA Ops:
  0.6 0.0 copy-start
  0.6 0.7 copy-done
  1.3 0.0 copy-start.1
  1.3 0.7 copy-done.1
  2.0 123.8 %selected_inversion.1 = (f32[2,256,256]{2,1,0:T(8,128)S(1)}, f32[2,256,256]{2,1,0:T(8,128)S(1)}) custom-call(s32[2]{0:T(128)S(1)} %copy-done.1, f32[2,2]{1,0:T(2,128)S(1)} %copy-done, f32[2,2,2,256,256]{4,3,2,1,0:T(8,128)} %p_hbm.1, f32[2,2,2,256,256]{4,3,2,1,0:T(8,128)} %f_hbm.1), custom_call_target="tpu_custom_call" | custom-call | tf_op jit(solution)/shard_map/selected_inversion/pallas_call | solution.py:556
  125.8 0.8 copy.8
  126.6 0.8 copy.9
Async XLA Ops:
  0.6 0.7 copy-start
  1.3 0.7 copy-start.1

commit v4 on v3

--- a/solution.py
+++ b/solution.py
@@ -213,50 +213,42 @@
             remote(out_b.at[p, out], got_b.at[p, level], p, 2 * (level // 2) + 1, 2 * level + 1, to),
         ]
 
-    def post_step(p, level, slot, a_pair):
+    def post_a(p, level, a_pair):
         out = 0 if level < 2 else 1
         out_a[p, out, 0] = a_pair[0]
         out_a[p, out, 1] = a_pair[1]
+
+    def post_b(p, level, slot):
+        out = 0 if level < 2 else 1
         pack2(out_b.at[p, out], (steps_b[p, slot, 0], steps_b[p, slot, 1]))
-        for copy in step_copies(p, level):
-            copy.start()
 
     def head_copies(p, src):
         n = m + 1
         forward = lax.rem(p + 1 - lax.rem(n, 2), 2) == 1
-        base = lax.rem(GROUP * n, nodes)
-        after = lax.rem(GROUP * (n + 1) + 3 * p, nodes)
-        to_oct = n == 4
-        to_head = forward & (n != 5) & (n < groups - 1)
-        to_pair = forward & (n < groups)
-        to_base = n < groups
-        oct_copy = remote(src.at[p], jump.at[p], p, 4, 6, after)
-        head_copy = remote(src.at[p], jump.at[p], p, 5, 6, base + 3)
-        pair = remote(src.at[p], jump.at[p], p, 6, 6, base + 1)
-        base_copy = remote(src.at[p], entry.at[p], p, 7, 7, base)
-        urgent = [
-            (to_oct, oct_copy),
-            (to_head & ~to_oct, head_copy),
-            (to_pair & ~to_head & ~to_oct, pair),
-            (to_base & ~to_pair & ~to_oct, base_copy),
+        base = GROUP * n
+        ahead = jnp.where(
+            n == 4, base + 4 + 3 * p, base + jnp.where((n == 5) | (n == groups - 1), 1, 3)
+        )
+        to_jump = (n < groups) & (forward | (n == 4))
+        to_entry = (n < groups) & ~to_jump
+        return [
+            (to_jump, remote(src.at[p], jump.at[p], p, 4, 6, lax.rem(ahead, nodes))),
+            (to_entry, remote(src.at[p], entry.at[p], p, 4, 7, lax.rem(base, nodes))),
+            ((n == 4) & forward, remote(src.at[p], jump.at[p], p, 6, 6, lax.rem(base + 3, nodes))),
+            ((n == 4) & ~forward, remote(src.at[p], entry.at[p], p, 6, 7, lax.rem(base, nodes))),
         ]
-        rest = [
-            (to_head & to_oct, head_copy),
-            (to_pair & (to_head | to_oct), pair),
-            (to_base & (to_pair | to_oct), base_copy),
+
+    def send_head(p, src):
+        for when, copy in head_copies(p, src):
+            pl.when(when)(copy.start)
+
+    def relay_copies(p):
+        to_jump = quads & ~upper & plus(p) & (g == 3)
+        to_entry = composing & plus(p) & (g == 1)
+        return [
+            (to_jump, remote(jump.at[p], jump.at[p], p, 5, 6, lax.rem(i + nodes - 2, nodes))),
+            (to_entry, remote(jump.at[p], entry.at[p], p, 5, 7, lax.rem(i + nodes - 1, nodes))),
         ]
-        return urgent, rest
-
-    def send_head(p, src):
-        for when, copy in head_copies(p, src)[0]:
-            pl.when(when)(copy.start)
-
-    def send_rest(p, src):
-        urgent, rest = head_copies(p, src)
-        for when, copy in urgent:
-            pl.when(when)(copy.wait_send)
-        for when, copy in rest:
-            pl.when(when)(copy.start)
 
     def pair_copy(p, ahead):
         return remote(pair_out.at[p], entry.at[p], p, 8, 7, lax.rem(i + ahead, nodes))
@@ -276,35 +268,75 @@
                 )
             real, imag = product(load4(fs.at[p, 0]), load4(fs.at[p, 1]))
             store4(steps_a.at[p, OWN], csplit((real, imag)))
+
+            if p == 0:
+
+                @pl.when(low == 0)
+                def _():
+                    pl.semaphore_wait(barrier, 2 * len(NEAR) + 7)
+
+            @pl.when(composing & first_sender(p))
+            def _():
+                post_a(p, 0, (real, imag))
+
+                @pl.when(low == 0)
+                def _():
+                    step_copies(p, 0)[0].start()
+
+        for p in range(2):
             loads[3 + 2 * p].wait()
             inner = sandwich(pivot(p, 0), load4(fs.at[p, 1]))
             last = pivot(p, 1)
             for part in range(2):
                 steps_b[p, OWN, part] = last[part] + inner[part]
 
-            if p == 0:
-                pl.semaphore_wait(barrier, 2 * len(NEAR) + 7)
-
             @pl.when(composing & first_sender(p))
             def _():
-                post_step(p, 0, OWN, (real, imag))
-
-    def merge(p, level, own, received, new, forward):
-        for copy in step_copies(p, level):
-            copy.wait_recv()
+                post_b(p, 0, OWN)
+
+                @pl.when(low == 0)
+                def _():
+                    step_copies(p, 0)[1].start()
+
+        @pl.when(low == 1)
+        def _():
+            pl.semaphore_wait(barrier, 2 * len(NEAR) + 7)
+            for p in range(2):
+
+                @pl.when(composing & first_sender(p))
+                def _():
+                    for copy in step_copies(p, 0):
+                        copy.start()
+
+
+    def merge(p, level, own, received, new, forward, sends):
+        copies = step_copies(p, level)
+        copies[0].wait_recv()
         store4(steps_a.at[p, received], csplit((got_a[p, level, 0], got_a[p, level, 1])))
+        first = jnp.where(forward, received, own)
+        second = jnp.where(forward, own, received)
+        a_pair = product(load4(steps_a.at[p, first]), load4(steps_a.at[p, second]))
+        store4(steps_a.at[p, new], csplit(a_pair))
+        if sends is not None:
+
+            @pl.when(sends)
+            def _():
+                post_a(p, level + 1, a_pair)
+                step_copies(p, level + 1)[0].start()
+
+        copies[1].wait_recv()
         block = unpack2(got_b.at[p, level])
         steps_b[p, received, 0] = block[0]
         steps_b[p, received, 1] = block[1]
-        first = jnp.where(forward, received, own)
-        second = jnp.where(forward, own, received)
-        outer = load4(steps_a.at[p, second])
-        inner = sandwich((steps_b[p, first, 0], steps_b[p, first, 1]), outer)
+        inner = sandwich((steps_b[p, first, 0], steps_b[p, first, 1]), load4(steps_a.at[p, second]))
         for part in range(2):
             steps_b[p, new, part] = steps_b[p, second, part] + inner[part]
-        a_pair = product(load4(steps_a.at[p, first]), outer)
-        store4(steps_a.at[p, new], csplit(a_pair))
-        return a_pair
+        if sends is not None:
+
+            @pl.when(sends)
+            def _():
+                post_b(p, level + 1, new)
+                step_copies(p, level + 1)[1].start()
 
     with jax.named_scope("pairs"):
 
@@ -313,11 +345,7 @@
             def body(p):
                 @pl.when(~first_sender(p))
                 def _():
-                    a_pair = merge(p, 0, OWN, GOT1, PAIR, plus(p))
-
-                    @pl.when(quads & second_sender(p))
-                    def _():
-                        post_step(p, 1, PAIR, a_pair)
+                    merge(p, 0, OWN, GOT1, PAIR, plus(p), quads & second_sender(p))
 
             both(body)
 
@@ -328,11 +356,7 @@
             def body(p):
                 @pl.when(head(p))
                 def _():
-                    a_pair = merge(p, 1, PAIR, GOT2, QUAD, plus(p))
-
-                    @pl.when(lower)
-                    def _():
-                        post_step(p, 2, QUAD, a_pair)
+                    merge(p, 1, PAIR, GOT2, QUAD, plus(p), lower)
 
             both(body)
 
@@ -343,7 +367,7 @@
             def body(p):
                 @pl.when(head(p))
                 def _():
-                    merge(p, 2, QUAD, GOT3, OCT, True)
+                    merge(p, 2, QUAD, GOT3, OCT, True, None)
 
             both(body)
 
@@ -361,6 +385,8 @@
             @pl.when(jumps(p))
             def _():
                 remote(jump.at[p], jump.at[p], p, 4, 6, i).wait_recv()
+                for when, copy in relay_copies(p):
+                    pl.when(when)(copy.start)
                 state = unpack2(jump.at[p])
 
                 @pl.when(g == 1)
@@ -372,7 +398,6 @@
                 def _():
                     advance(p, jnp.where(upper, OCT, QUAD), state, head_out.at[p])
                     send_head(p, head_out)
-                    send_rest(p, head_out)
 
         both(body)
 
@@ -387,17 +412,25 @@
             device_id_type=MESH,
         )
 
-    def send_total(k, step):
-        to = lax.rem(me + step, 8)
-        rows = pl.ds(pl.multiple_of(me * PART, 8), PART)
+    sibling = me + 1 - 2 * lax.rem(me, 2)
+
+    def send_total(k, owner, to, slot):
+        rows = pl.ds(pl.multiple_of(owner * PART, 8), PART)
         return pltpu.make_async_remote_copy(
             src_ref=total.at[k, rows],
             dst_ref=total.at[k, rows],
-            send_sem=ag_send.at[k, step - 1],
-            recv_sem=ag_recv.at[k, step - 1],
+            send_sem=ag_send.at[k, slot],
+            recv_sem=ag_recv.at[k, slot],
             device_id=(to, i),
             device_id_type=MESH,
         )
+
+    def same_core(step):
+        return lax.rem(me + step, 8)
+
+    def first_totals(k):
+        copies = [send_total(k, me, same_core(step), step - 1) for step in (4, 2, 6)]
+        return copies + [send_total(k, me, sibling, 0)]
 
     order = (4, 3, 5, 2, 6, 7, 1)
 
@@ -422,7 +455,9 @@
     loads[1].wait()
     passes_on = (m == 0) | (lax.rem(g, 2) == 0)
 
-    def enter(p):
+    later = composing & (g == 0)
+
+    def enter(p, hold):
         @pl.when(i == 0)
         def _():
             s_in[p] = jnp.zeros_like(s_in[p])
@@ -450,18 +485,13 @@
         def _():
             advance(p, OWN, (s_in[p, 0], s_in[p, 1]), own_out.at[p])
 
-            @pl.when((m > 0) | (g < 3))
+            @pl.when(((m > 0) | (g < 3)) & ~(later & hold))
             def _():
                 own_copy(p).start()
 
             @pl.when((m == 0) & (g == 3))
             def _():
                 send_head(p, own_out)
-                send_rest(p, own_out)
-
-        @pl.when(quads & ~upper & (g == 0) & ~plus(p))
-        def _():
-            send_rest(p, head_out)
 
     def details(n, p):
         state = (s_in[p, 0], s_in[p, 1])
@@ -475,15 +505,19 @@
 
     with jax.named_scope("states"):
         one, two = lax.rem(low, 2), lax.rem(low + 1, 2)
-        enter(one)
-
-        @pl.when(~passes_on)
+        enter(one, True)
+
+        @pl.when(~passes_on | later)
         def _():
             details(0, one)
 
-        enter(two)
-
-        @pl.when(passes_on)
+            @pl.when(later)
+            def _():
+                own_copy(one).start()
+
+        enter(two, False)
+
+        @pl.when(passes_on & ~later)
         def _():
             details(0, one)
 
@@ -498,21 +532,20 @@
                 send_part(k, step).wait_recv()
                 acc = acc + parts[k, step - 1]
             total[k, mine] = acc
-            for step in order:
-                send_total(k, step).start()
+            for copy in first_totals(k):
+                copy.start()
     with jax.named_scope("pole_gather"):
+        def pass_on(k, step):
+            return send_total(k, lax.rem(me + 8 - step, 8), sibling, step)
+
         for k in range(2):
-            for step in range(1, 8):
-                back = lax.rem(me + 8 - step, 8)
-                rows = pl.ds(pl.multiple_of(back * PART, 8), PART)
-                pltpu.make_async_remote_copy(
-                    src_ref=total.at[k, rows],
-                    dst_ref=total.at[k, rows],
-                    send_sem=ag_send.at[k, step - 1],
-                    recv_sem=ag_recv.at[k, step - 1],
-                    device_id=(back, i),
-                    device_id_type=MESH,
-                ).wait_recv()
+            for step in (2, 6, 4):
+                send_total(k, lax.rem(me + 8 - step, 8), me, step - 1).wait_recv()
+                pass_on(k, step).start()
+        for k in range(2):
+            send_total(k, sibling, me, 0).wait_recv()
+            for step in (2, 6, 4):
+                send_total(k, lax.rem(sibling + 8 - step, 8), me, step).wait_recv()
             off_ref[k, :, 0:H] = total[k, 0:W]
             off_ref[k, :, H:W] = total[k, W : 2 * W]
             diag_ref[k] = unpack(total.at[k, pl.ds(2 * W, PACK)])
@@ -530,8 +563,11 @@
 
         @pl.when((quads & head(p)) | ((m == 0) & (g == 3)))
         def _():
-            for when, copy in head_copies(p, head_out)[1]:
+            for when, copy in head_copies(p, head_out):
                 pl.when(when)(copy.wait_send)
+
+        for when, copy in relay_copies(p):
+            pl.when(when)(copy.wait_send)
 
         @pl.when(composing & ((plus(p) & (g == 1)) | (~plus(p) & (g == 0))))
         def _():
@@ -545,12 +581,15 @@
     for k in range(2):
         for step in range(1, 8):
             send_part(k, step).wait_send()
-            send_total(k, step).wait_send()
+        for copy in first_totals(k):
+            copy.wait_send()
+        for step in (2, 6, 4):
+            pass_on(k, step).wait_send()
 
 
 def local(nodes, pivot_inverse, factor_block, live_width_array, pole_weight):
     vmem = pl.BlockSpec(memory_space=pltpu.VMEM)
-    hbm = pl.BlockSpec(memory_space=pl.ANY)
+    hbm = pl.BlockSpec(memory_space=pltpu.HBM)
     dma = pltpu.SemaphoreType.DMA
     packed = pltpu.VMEM((2, 2, PACK, H), F32)
     return pl.pallas_call(

time: 130 us -> 122 us (0.938)
  Pallas kernels: 124 us -> 117 us
    pallas_call x1, Pallas kernels: 124 us -> 117 us  [local(): pl.pallas_call(functools.partial(kernel, nodes), out_shape=[jax.ShapeDtyp...]
where the time goes in v4:
time: 122 us; the launch traced here: 121 us
  Pallas kernels  117 us (96%)
  local copies, waits for them, and re-layouts  2.92 us (2%)
    pallas_call x1, Pallas kernels, local(): pl.pallas_call(functools.partial(kernel, nodes), out_shape=[jax.ShapeDtyp...  117 us
    unnamed x6, local copies, waits for them, and re-layouts  2.92 us

profile of v4, /device:TPU:167, one launch (start us, length us, event | category | flops | bytes accessed | tf_op | source)
XLA Modules:
  0.0 120.6 jit_solution(7601063872850829114)
XLA Ops:
  0.6 0.0 copy-start
  0.6 0.7 copy-done
  1.3 0.0 copy-start.1
  1.3 0.7 copy-done.1
  2.0 117.1 %selected_inversion.1 = (f32[2,256,256]{2,1,0:T(8,128)S(1)}, f32[2,256,256]{2,1,0:T(8,128)S(1)}) custom-call(s32[2]{0:T(128)S(1)} %copy-done.1, f32[2,2]{1,0:T(2,128)S(1)} %copy-done, f32[2,2,2,256,256]{4,3,2,1,0:T(8,128)} %p_hbm.1, f32[2,2,2,256,256]{4,3,2,1,0:T(8,128)} %f_hbm.1), custom_call_target="tpu_custom_call" | custom-call | tf_op jit(solution)/shard_map/selected_inversion/pallas_call | solution.py:595
  119.0 0.8 copy.8
  119.8 0.8 copy.9
Async XLA Ops:
  0.6 0.7 copy-start
  1.3 0.7 copy-start.1

commit v5 on v4

--- a/solution.py
+++ b/solution.py
@@ -17,7 +17,7 @@
 ROWS = 8 * PART
 GROUP = 4
 VMEM_MIB = 52
-OWN, GOT1, PAIR, GOT2, QUAD, GOT3, OCT = range(7)
+OWN, GOT1, PAIR, GOT2, QUAD, GOT3, OCT, AHEAD, AHEAD8 = range(9)
 NEAR = (1, 2, 4, 5, 7, 8)
 
 
@@ -127,6 +127,7 @@
     ag_recv,
 ):
     me = lax.axis_index("pole")
+    core = lax.rem(me, 2)
     i = lax.axis_index("snode")
     groups = nodes // GROUP
     g = lax.rem(i, GROUP)
@@ -187,8 +188,18 @@
 
     composing = m > 0
     quads = composing & (m < groups - 1)
+    final = m == groups - 1
     lower = m == 4
     upper = m == 5
+
+    def second(p):
+        return quads | (final & plus(p))
+
+    def direct(p):
+        return composing & plus(p) & ((g == 3) | (g == 1))
+
+    def passes(p):
+        return (m == 0) | (((g == 0) | (g == 2)) & ~plus(p))
 
     def remote(src, dst, p, kind, landing, to):
         return pltpu.make_async_remote_copy(
@@ -230,11 +241,13 @@
             n == 4, base + 4 + 3 * p, base + jnp.where((n == 5) | (n == groups - 1), 1, 3)
         )
         to_jump = (n < groups) & (forward | (n == 4))
+        final_next = n == groups - 1
         to_entry = (n < groups) & ~to_jump
         return [
             (to_jump, remote(src.at[p], jump.at[p], p, 4, 6, lax.rem(ahead, nodes))),
             (to_entry, remote(src.at[p], entry.at[p], p, 4, 7, lax.rem(base, nodes))),
             ((n == 4) & forward, remote(src.at[p], jump.at[p], p, 6, 6, lax.rem(base + 3, nodes))),
+            (final_next & forward, remote(src.at[p], jump.at[p], p, 6, 6, lax.rem(base + 3, nodes))),
             ((n == 4) & ~forward, remote(src.at[p], entry.at[p], p, 6, 7, lax.rem(base, nodes))),
         ]
 
@@ -345,35 +358,45 @@
             def body(p):
                 @pl.when(~first_sender(p))
                 def _():
-                    merge(p, 0, OWN, GOT1, PAIR, plus(p), quads & second_sender(p))
+                    merge(p, 0, OWN, GOT1, PAIR, plus(p), second(p) & second_sender(p))
 
             both(body)
 
     with jax.named_scope("quads"):
 
-        @pl.when(quads)
+        @pl.when(composing)
+        def _():
+            def body(p):
+                @pl.when(second(p) & head(p))
+                def _():
+                    merge(p, 1, PAIR, GOT2, QUAD, plus(p), lower)
+
+            both(body)
+
+    with jax.named_scope("octs"):
+
+        @pl.when(upper)
         def _():
             def body(p):
                 @pl.when(head(p))
                 def _():
-                    merge(p, 1, PAIR, GOT2, QUAD, plus(p), lower)
+                    merge(p, 2, QUAD, GOT3, OCT, True, None)
 
             both(body)
 
-    with jax.named_scope("octs"):
-
-        @pl.when(upper)
-        def _():
-            def body(p):
-                @pl.when(head(p))
-                def _():
-                    merge(p, 2, QUAD, GOT3, OCT, True, None)
-
-            both(body)
+    def advanced(p, slot, state):
+        inner = sandwich(state, load4(steps_a.at[p, slot]))
+        return steps_b[p, slot, 0] + inner[0], steps_b[p, slot, 1] + inner[1]
 
     def advance(p, slot, state, ref):
-        inner = sandwich(state, load4(steps_a.at[p, slot]))
-        pack2(ref, (steps_b[p, slot, 0] + inner[0], steps_b[p, slot, 1] + inner[1]))
+        pack2(ref, advanced(p, slot, state))
+
+    def compose(p, first, second, new):
+        outer = load4(steps_a.at[p, second])
+        store4(steps_a.at[p, new], csplit(product(load4(steps_a.at[p, first]), outer)))
+        inner = sandwich((steps_b[p, first, 0], steps_b[p, first, 1]), outer)
+        for part in range(2):
+            steps_b[p, new, part] = steps_b[p, second, part] + inner[part]
 
     def jumps(p):
         forward = plus(p) & ((g == 1) | ((g == 3) & quads))
@@ -398,6 +421,19 @@
                 def _():
                     advance(p, jnp.where(upper, OCT, QUAD), state, head_out.at[p])
                     send_head(p, head_out)
+
+        both(body)
+
+    with jax.named_scope("steps_ahead"):
+
+        def body(p):
+            @pl.when(direct(p) & (g == 3))
+            def _():
+                compose(p, GOT2, GOT1, AHEAD)
+
+                @pl.when(upper)
+                def _():
+                    compose(p, GOT3, AHEAD, AHEAD8)
 
         both(body)
 
@@ -412,7 +448,7 @@
             device_id_type=MESH,
         )
 
-    sibling = me + 1 - 2 * lax.rem(me, 2)
+    sibling = me + 1 - 2 * core
 
     def send_total(k, owner, to, slot):
         rows = pl.ds(pl.multiple_of(owner * PART, 8), PART)
@@ -453,7 +489,6 @@
                 send_part(k, step).start()
 
     loads[1].wait()
-    passes_on = (m == 0) | (lax.rem(g, 2) == 0)
 
     later = composing & (g == 0)
 
@@ -464,13 +499,24 @@
             pack2(own_out.at[p], (steps_b[p, OWN, 0], steps_b[p, OWN, 1]))
             own_copy(p).start()
 
-        @pl.when(i > 0)
+        @pl.when((i > 0) & ~direct(p))
         def _():
             remote(entry.at[p], entry.at[p], p, 7, 7, i).wait_recv()
             block = unpack2(entry.at[p])
             s_in[p, 0] = block[0]
             s_in[p, 1] = block[1]
 
+        @pl.when(direct(p))
+        def _():
+            @pl.when(final & (g == 3))
+            def _():
+                remote(jump.at[p], jump.at[p], p, 4, 6, i).wait_recv()
+
+            slot = jnp.where(g == 1, GOT1, jnp.where(upper, AHEAD8, AHEAD))
+            block = advanced(p, slot, unpack2(jump.at[p]))
+            s_in[p, 0] = block[0]
+            s_in[p, 1] = block[1]
+
         @pl.when(composing & (g == 0) & ~plus(p))
         def _():
             @pl.when(quads & ~upper)
@@ -481,7 +527,7 @@
             advance(p, PAIR, (s_in[p, 0], s_in[p, 1]), pair_out.at[p])
             pair_copy(p, 2).start()
 
-        @pl.when(passes_on & (i > 0))
+        @pl.when(passes(p) & (i > 0))
         def _():
             advance(p, OWN, (s_in[p, 0], s_in[p, 1]), own_out.at[p])
 
@@ -504,25 +550,30 @@
             put(n, p, k, moved, state)
 
     with jax.named_scope("states"):
-        one, two = lax.rem(low, 2), lax.rem(low + 1, 2)
+        flip = jnp.where(composing, lax.rem(g, 2), 0)
+        one, two = lax.rem(low + flip, 2), lax.rem(low + flip + 1, 2)
         enter(one, True)
 
-        @pl.when(~passes_on | later)
+        @pl.when(composing)
         def _():
             details(0, one)
 
-            @pl.when(later)
+            @pl.when(later & (core == 0))
             def _():
                 own_copy(one).start()
 
         enter(two, False)
 
-        @pl.when(passes_on & ~later)
+        @pl.when(m == 0)
         def _():
             details(0, one)
 
     with jax.named_scope("last_details"):
         details(1, two)
+
+        @pl.when(later & (core == 1))
+        def _():
+            own_copy(one).start()
 
     with jax.named_scope("pole_sum"):
         mine = pl.ds(pl.multiple_of(me * PART, 8), PART)
@@ -551,7 +602,7 @@
             diag_ref[k] = unpack(total.at[k, pl.ds(2 * W, PACK)])
 
     def body(p):
-        @pl.when(composing & (first_sender(p) | (quads & second_sender(p))))
+        @pl.when(composing & (first_sender(p) | (second(p) & second_sender(p))))
         def _():
             for copy in step_copies(p, 0):
                 copy.wait_send()
@@ -573,7 +624,7 @@
         def _():
             pair_copy(p, 1).wait_send()
 
-        @pl.when(passes_on & ((m > 0) | (g < 3)))
+        @pl.when(passes(p) & ((m > 0) | (g < 3)))
         def _():
             own_copy(p).wait_send()
 
@@ -603,8 +654,8 @@
             pltpu.SMEM((2,), jnp.int32),
             pltpu.SMEM((2, 2), F32),
             pltpu.VMEM((2, 2, 4, W, W), BF),
-            pltpu.VMEM((2, 7, 4, W, W), BF),
-            pltpu.VMEM((2, 7, 2, W, W), F32),
+            pltpu.VMEM((2, 9, 4, W, W), BF),
+            pltpu.VMEM((2, 9, 2, W, W), F32),
             pltpu.VMEM((2, 3, 2, W, W), F32),
             pltpu.VMEM((2, 3, 2, PACK, H), F32),
             pltpu.VMEM((2, 2, 2, W, W), F32),

time: 122 us -> 119 us (0.975)
  Pallas kernels: 117 us -> 115 us
    pallas_call x1, Pallas kernels: 117 us -> 115 us  [local(): pl.pallas_call(functools.partial(kernel, nodes), out_shape=[jax.ShapeDtyp...]
where the time goes in v5:
time: 119 us
  Pallas kernels  115 us (97%)
  local copies, waits for them, and re-layouts  2.92 us (2%)
    pallas_call x1, Pallas kernels, local(): pl.pallas_call(functools.partial(kernel, nodes), out_shape=[jax.ShapeDtyp...  115 us
    unnamed x6, local copies, waits for them, and re-layouts  2.92 us

profile of v5, /device:TPU:167, one launch (start us, length us, event | category | flops | bytes accessed | tf_op | source)
XLA Modules:
  0.0 118.6 jit_solution(8524999394124431833)
XLA Ops:
  0.6 0.0 copy-start
  0.6 0.7 copy-done
  1.3 0.0 copy-start.1
  1.3 0.7 copy-done.1
  2.0 115.0 %selected_inversion.1 = (f32[2,256,256]{2,1,0:T(8,128)S(1)}, f32[2,256,256]{2,1,0:T(8,128)S(1)}) custom-call(s32[2]{0:T(128)S(1)} %copy-done.1, f32[2,2]{1,0:T(2,128)S(1)} %copy-done, f32[2,2,2,256,256]{4,3,2,1,0:T(8,128)} %p_hbm.1, f32[2,2,2,256,256]{4,3,2,1,0:T(8,128)} %f_hbm.1), custom_call_target="tpu_custom_call" | custom-call | tf_op jit(solution)/shard_map/selected_inversion/pallas_call | solution.py:646
  117.0 0.8 copy.8
  117.8 0.8 copy.9
Async XLA Ops:
  0.6 0.7 copy-start
  1.3 0.7 copy-start.1

commit v6 on v5

--- a/solution.py
+++ b/solution.py
@@ -351,12 +351,74 @@
                 post_b(p, level + 1, new)
                 step_copies(p, level + 1)[1].start()
 
+    def take_a(p, level, received):
+        step_copies(p, level)[0].wait_recv()
+        store4(steps_a.at[p, received], csplit((got_a[p, level, 0], got_a[p, level, 1])))
+
+    def take_b(p, level, received):
+        step_copies(p, level)[1].wait_recv()
+        block = unpack2(got_b.at[p, level])
+        steps_b[p, received, 0] = block[0]
+        steps_b[p, received, 1] = block[1]
+
+    def inner_into(p, first, second, new):
+        inner = sandwich((steps_b[p, first, 0], steps_b[p, first, 1]), load4(steps_a.at[p, second]))
+        steps_b[p, new, 0] = inner[0]
+        steps_b[p, new, 1] = inner[1]
+
+    def add_into(p, extra, new):
+        for part in range(2):
+            steps_b[p, new, part] += steps_b[p, extra, part]
+
+    def gather(p):
+        ahead = plus(p)
+        take_a(p, 0, GOT1)
+        first, second = jnp.where(ahead, GOT1, OWN), jnp.where(ahead, OWN, GOT1)
+        pair = product(load4(steps_a.at[p, first]), load4(steps_a.at[p, second]))
+        store4(steps_a.at[p, PAIR], csplit(pair))
+
+        @pl.when(~ahead)
+        def _():
+            inner_into(p, OWN, GOT1, PAIR)
+
+        take_a(p, 1, GOT2)
+        first, second = jnp.where(ahead, GOT2, PAIR), jnp.where(ahead, PAIR, GOT2)
+        quad = product(load4(steps_a.at[p, first]), load4(steps_a.at[p, second]))
+        store4(steps_a.at[p, QUAD], csplit(quad))
+
+        @pl.when(lower)
+        def _():
+            post_a(p, 2, quad)
+            step_copies(p, 2)[0].start()
+
+        @pl.when(ahead)
+        def _():
+            take_b(p, 1, GOT2)
+            inner_into(p, GOT2, PAIR, QUAD)
+            take_b(p, 0, GOT1)
+            inner_into(p, GOT1, OWN, PAIR)
+            add_into(p, OWN, PAIR)
+            add_into(p, PAIR, QUAD)
+
+        @pl.when(~ahead)
+        def _():
+            take_b(p, 0, GOT1)
+            add_into(p, GOT1, PAIR)
+            inner_into(p, PAIR, GOT2, QUAD)
+            take_b(p, 1, GOT2)
+            add_into(p, GOT2, QUAD)
+
+        @pl.when(lower)
+        def _():
+            post_b(p, 2, QUAD)
+            step_copies(p, 2)[1].start()
+
     with jax.named_scope("pairs"):
 
         @pl.when(composing)
         def _():
             def body(p):
-                @pl.when(~first_sender(p))
+                @pl.when(~first_sender(p) & ~(second(p) & head(p)))
                 def _():
                     merge(p, 0, OWN, GOT1, PAIR, plus(p), second(p) & second_sender(p))
 
@@ -369,7 +431,7 @@
             def body(p):
                 @pl.when(second(p) & head(p))
                 def _():
-                    merge(p, 1, PAIR, GOT2, QUAD, plus(p), lower)
+                    gather(p)
 
             both(body)
 

time: 119 us -> 116 us (0.975)
  Pallas kernels: 115 us -> 112 us
    pallas_call x1, Pallas kernels: 115 us -> 112 us  [local(): pl.pallas_call(functools.partial(kernel, nodes), out_shape=[jax.ShapeDtyp...]
where the time goes in v6:
time: 116 us; the launch traced here: 115 us
  Pallas kernels  112 us (97%)
  local copies, waits for them, and re-layouts  2.92 us (3%)
    pallas_call x1, Pallas kernels, local(): pl.pallas_call(functools.partial(kernel, nodes), out_shape=[jax.ShapeDtyp...  112 us
    unnamed x6, local copies, waits for them, and re-layouts  2.92 us

profile of v6, /device:TPU:167, one launch (start us, length us, event | category | flops | bytes accessed | tf_op | source)
XLA Modules:
  0.0 115.5 jit_solution(7536015603346083766)
XLA Ops:
  0.6 0.0 copy-start
  0.6 0.7 copy-done
  1.3 0.0 copy-start.1
  1.3 0.7 copy-done.1
  2.0 111.9 %selected_inversion.1 = (f32[2,256,256]{2,1,0:T(8,128)S(1)}, f32[2,256,256]{2,1,0:T(8,128)S(1)}) custom-call(s32[2]{0:T(128)S(1)} %copy-done.1, f32[2,2]{1,0:T(2,128)S(1)} %copy-done, f32[2,2,2,256,256]{4,3,2,1,0:T(8,128)} %p_hbm.1, f32[2,2,2,256,256]{4,3,2,1,0:T(8,128)} %f_hbm.1), custom_call_target="tpu_custom_call" | custom-call | tf_op jit(solution)/shard_map/selected_inversion/pallas_call | solution.py:708
  113.9 0.8 copy.8
  114.7 0.8 copy.9
Async XLA Ops:
  0.6 0.7 copy-start
  1.3 0.7 copy-start.1
